TPU v7x, 128 devices: a whole 4x4x4 slice. The times are simulated.
128 devices in a mesh: node: 4 (over y), local: 32 (over x, z, core).
Axes of the slice: x: 4, y: 4, z: 4, core: 2. Of those that a mesh axis runs over, the one named last changes fastest.
Arguments:
- tokens: bfloat16 [16384, 7168], P(('node', 'local')), may hold values from -6 to 6
- route_ids: int32 [16384, 8], P(('node', 'local')), may hold values from 0 to 383, all different within a row; in each aligned block of 128 rows (0 to 127, 128 to 255, ...) at most 5 rows name the same one
- route_gates: bfloat16 [16384, 8], P(('node', 'local')), may hold values from 0.099609375 to 1
- limits: int32 [384], replicated, may hold values from 1 to 5, as said below
- w_gate: bfloat16 [128, 7168, 448], P(('node', 'local')), may hold values from -0.0625 to 0.0625
- w_up: bfloat16 [128, 7168, 448], P(('node', 'local')), may hold values from -0.0625 to 0.0625
- w_down: bfloat16 [128, 448, 7168], P(('node', 'local')), may hold values from -0.125 to 0.125
Outputs:
- mixed: bfloat16 [16384, 7168], P(('node', 'local'))
Inputs may be any that keep to these rules, and one draw needn't show every extreme that they name: `route_ids`: in each aligned block of 128 rows (the rows of one device) no expert is named by more than 5 rows, a bound that some block reaches; a row names 8 different experts. `limits`: some expert's capacity is exactly 5.
All inputs are finite; a program needn't handle non-finite values.
Results may differ from a plain program's by a relative error of at most 0.0057.
Values may be sent and summed in bfloat16 or wider, within the bound.
No kernel may reach another device: no remote copies, remote signals or barrier semaphores. Data moves between devices by JAX's collectives and lax.ppermute only.
A program may use at most 128 MiB of HBM per device.

v0:
```python
import jax
import jax.numpy as jnp
from jax import lax
from jax.sharding import PartitionSpec as P

GROUP = 4
CAP = 5


def slab_output(packed, gate_slab, up_slab, down_slab):
    flat_rows = packed.reshape(-1, packed.shape[-1])
    gate_act = jnp.dot(flat_rows, gate_slab, preferred_element_type=jnp.float32)
    upper = jnp.dot(flat_rows, up_slab, preferred_element_type=jnp.float32)
    hidden = (jax.nn.silu(gate_act) * upper).astype(jnp.bfloat16)
    result = jnp.dot(hidden, down_slab, preferred_element_type=jnp.float32).astype(jnp.bfloat16)
    return result.reshape(packed.shape[:-1] + (down_slab.shape[1],))


def routing(route_ids, route_gates, limits, hosted):
    experts = jnp.arange(hosted, dtype=jnp.int32)
    matches = route_ids[:, :, None] == experts[None, None, :]
    per_tok = jnp.sum(matches.astype(jnp.int32), axis=1)
    before = jnp.cumsum(per_tok, axis=0) - per_tok
    keep_mask = (per_tok > 0) & (before < limits[None, :hosted])
    gate_sum = jnp.sum(jnp.where(matches, route_gates.astype(jnp.float32)[:, :, None], 0.0), axis=1)
    return (keep_mask, before, jnp.where(keep_mask, gate_sum, 0.0))


def on_device(tokens, route_ids, route_gates, limits, w_gate, w_up, w_down):
    node_count = lax.axis_size("node")
    local_count = lax.axis_size("local")
    exp_node = local_count // GROUP
    hosted = node_count * exp_node
    tok_rows = tokens.shape[0]
    width = tokens.shape[1]
    keep_mask, before, weights = routing(route_ids, route_gates, limits, hosted)
    gate_slab, up_slab, down_slab = (w_gate[0], w_up[0], w_down[0])
    capacity = jnp.arange(CAP, dtype=jnp.int32)
    node_rows = min(tok_rows, exp_node * CAP)
    kept_nodes = keep_mask.reshape(tok_rows, node_count, exp_node)
    needed = jnp.any(kept_nodes, axis=2)
    needed_int = needed.astype(jnp.int32)
    position = jnp.cumsum(needed_int, axis=0) - needed_int
    slots = jnp.arange(node_rows, dtype=jnp.int32)
    placed = needed[:, :, None] & (position[:, :, None] == slots[None, None, :])
    rows_out = jnp.einsum(
        "tms,td->msd", placed.astype(jnp.bfloat16), tokens, preferred_element_type=jnp.float32
    ).astype(jnp.bfloat16)
    rank_tok = (jnp.where(keep_mask, before, -1) + 1).reshape(tok_rows, node_count, exp_node)
    ranks_out = jnp.einsum("tms,tmg->msg", placed.astype(jnp.int32), rank_tok) - 1
    gates_out = jnp.einsum(
        "tms,tmg->msg",
        placed.astype(jnp.float32),
        weights.reshape(tok_rows, node_count, exp_node),
        precision=lax.Precision.HIGHEST,
    ).astype(jnp.bfloat16)
    rows_in, gates_in, ranks_in = (
        lax.all_to_all(rows_out, "node", split_axis=0, concat_axis=0, tiled=True),
        lax.all_to_all(gates_out, "node", split_axis=0, concat_axis=0, tiled=True),
        lax.all_to_all(ranks_out, "node", split_axis=0, concat_axis=0, tiled=True),
    )
    matched = ranks_in[:, :, :, None] == capacity[None, None, None, :]
    forward = jnp.einsum(
        "nrgc,nrd->gncd", matched.astype(jnp.bfloat16), rows_in, preferred_element_type=jnp.float32
    ).astype(jnp.bfloat16)
    forward = jnp.broadcast_to(forward[:, None], (exp_node, GROUP, node_count, CAP, width)).reshape(
        local_count, node_count, CAP, width
    )
    returned = lax.all_to_all(
        slab_output(
            lax.all_to_all(forward, "local", split_axis=0, concat_axis=0, tiled=True),
            gate_slab,
            up_slab,
            down_slab,
        ),
        "local",
        split_axis=0,
        concat_axis=0,
        tiled=True,
    )
    summed = jnp.sum(
        returned.astype(jnp.float32).reshape(exp_node, GROUP, node_count, CAP, width), axis=1
    )
    combine = jnp.where(matched, gates_in.astype(jnp.float32)[:, :, :, None], 0.0)
    merged = jnp.einsum("nrgc,gncd->nrd", combine, summed, precision=lax.Precision.HIGHEST)
    gathered_back = lax.all_to_all(
        merged.astype(jnp.bfloat16), "node", split_axis=0, concat_axis=0, tiled=True
    ).astype(merged.dtype)
    mixed = jnp.einsum(
        "tms,msd->td", placed.astype(jnp.float32), gathered_back, precision=lax.Precision.HIGHEST
    )
    return mixed.astype(jnp.bfloat16)


def solution(mesh):
    return jax.shard_map(
        on_device,
        mesh=mesh,
        in_specs=(
            P(("node", "local"), None),
            P(("node", "local"), None),
            P(("node", "local"), None),
            P(),
            P(("node", "local"), None, None),
            P(("node", "local"), None, None),
            P(("node", "local"), None, None),
        ),
        out_specs=P(("node", "local"), None),
        check_vma=False,
    )
```

profile of v0, /device:TPU:36, one launch (start us, length us, event | category | flops | bytes accessed | tf_op | source)
XLA Modules:
  0.0 495.8 jit_solution(13926451666556989730)
XLA Ops:
  3.4 4.5 all-to-all-start
  7.9 2.1 convolution_convert_fusion.2
  10.0 3.2 all-to-all-done
  13.2 4.5 all-to-all-start.2
  18.9 26.1 %all-to-all-done.2 = bf16[4,40,7168]{2,1,0:T(8,128)(2,1)} async-done(((bf16[4,40,7168]{2,1,0:T(8,128)(2,1)}), bf16[4,40,7168]{2,1,0:T(8,128)(2,1)}, u32[]{:S(2)}, u32[]{:S(2)}) %all-to-all-start.2) | async-done | bytes 2293792 | tf_op jit(solution)/shard_map/all_to_all | solution.py:58
  45.0 2.4 fusion.2
  47.4 1.8 copy.76
  49.2 4.5 broadcast_in_dim.54
  53.7 8.2 %all-to-all-start.3 = ((bf16[32,4,5,7168]{3,1,2,0:T(4,128)(2,1)}), bf16[32,4,5,7168]{3,1,2,0:T(4,128)(2,1)}, u32[]{:S(2)}, u32[]{:S(2)}) async-start(bf16[32,4,5,7168]{3,1,2,0:T(4,128)(2,1)} %bitcast.62), calls=%async_computation.3 | async-start | bytes 18350080 | tf_op jit(solution)/shard_map/all_to_all | solution.py:71
  62.8 141.5 %all-to-all-done.3 = bf16[32,4,5,7168]{3,1,2,0:T(4,128)(2,1)} async-done(((bf16[32,4,5,7168]{3,1,2,0:T(4,128)(2,1)}), bf16[32,4,5,7168]{3,1,2,0:T(4,128)(2,1)}, u32[]{:S(2)}, u32[]{:S(2)}) %all-to-all-start.3) | async-done | bytes 9175072 | tf_op jit(solution)/shard_map/all_to_all | solution.py:71
  204.2 3.4 all-to-all-start.1
  207.7 13.7 %copy.77 = bf16[32,4,5,7168]{3,2,1,0:T(8,128)(2,1)} copy(bf16[32,4,5,7168]{3,1,2,0:T(4,128)(2,1)} %all-to-all-done.3) | data formatting | bytes 18350080 | tf_op jit(solution)/shard_map/all_to_all | solution.py:71
  221.4 15.1 %reshape.65 = bf16[640,7168]{1,0:T(8,128)(2,1)} reshape(bf16[32,4,5,7168]{3,2,1,0:T(8,128)(2,1)} %copy.77) | data formatting | bytes 18350080 | tf_op jit(solution)/shard_map/reshape | solution.py:11
  236.4 12.1 %fusion.6 = f32[640,448]{0,1:T(8,128)S(1)} fusion(bf16[640,7168]{1,0:T(8,128)(2,1)} %reshape.65, bf16[1,7168,448]{1,2,0:T(8,128)(2,1)} %param.11), kind=kOutput, calls=%fused_computation.12 | convolution fusion | flops 4110417920 | bytes 16744448 | tf_op jit(solution)/shard_map/dot_general | solution.py:12
  248.6 8.7 %fusion.14 = bf16[640,448]{0,1:T(8,128)(2,1)S(1)} fusion(bf16[640,7168]{1,0:T(8,128)(2,1)S(1)} %copy-done.2, bf16[1,7168,448]{1,2,0:T(8,128)(2,1)} %param.12, f32[640,448]{0,1:T(8,128)S(1)} %fusion.6), kind=kOutput, calls=%fused_computation.18 | convolution fusion | flops 4112138240 | bytes 17317888 | tf_op jit(solution)/shard_map/dot_general | solution.py:13
  257.3 11.3 %convolution_convert_fusion = bf16[640,7168]{1,0:T(8,128)(2,1)} fusion(bf16[640,448]{0,1:T(8,128)(2,1)S(1)} %fusion.14, bf16[1,448,7168]{2,1,0:T(8,128)(2,1)} %param.13), kind=kOutput, calls=%fused_computation.1 | convolution fusion | flops 4115005440 | bytes 16171008 | tf_op jit(solution)/shard_map/dot_general | solution.py:15
  268.6 14.8 %reshape.66 = bf16[32,4,5,7168]{3,2,1,0:T(8,128)(2,1)} reshape(bf16[640,7168]{1,0:T(8,128)(2,1)} %convolution_convert_fusion) | data formatting | bytes 18350080 | tf_op jit(solution)/shard_map/reshape | solution.py:16
  283.4 14.0 %copy.78 = bf16[32,4,5,7168]{3,1,2,0:T(4,128)(2,1)} copy(bf16[32,4,5,7168]{3,2,1,0:T(8,128)(2,1)} %reshape.66) | data formatting | bytes 18350080 | tf_op jit(solution)/shard_map/reshape | solution.py:16
  297.4 5.9 %all-to-all-start.4 = ((bf16[32,4,5,7168]{3,1,2,0:T(4,128)(2,1)}), bf16[32,4,5,7168]{3,1,2,0:T(4,128)(2,1)}, u32[]{:S(2)}, u32[]{:S(2)}) async-start(bf16[32,4,5,7168]{3,1,2,0:T(4,128)(2,1)} %copy.78), calls=%async_computation.4 | async-start | bytes 18350080 | tf_op jit(solution)/shard_map/all_to_all | solution.py:69
  303.4 142.3 %all-to-all-done.4 = bf16[32,4,5,7168]{3,1,2,0:T(4,128)(2,1)} async-done(((bf16[32,4,5,7168]{3,1,2,0:T(4,128)(2,1)}), bf16[32,4,5,7168]{3,1,2,0:T(4,128)(2,1)}, u32[]{:S(2)}, u32[]{:S(2)}) %all-to-all-start.4) | async-done | bytes 9175072 | tf_op jit(solution)/shard_map/all_to_all | solution.py:69
  445.7 9.3 %convert_reduce_fusion = f32[8,4,5,7168]{3,1,2,0:T(4,128)S(1)} fusion(bf16[32,4,5,7168]{3,1,2,0:T(4,128)(2,1)} %all-to-all-done.4), kind=kLoop, calls=%fused_computation | loop fusion | flops 8028160 | bytes 13762560 | tf_op jit(solution)/shard_map/reduce_sum | solution.py:81
  455.1 6.2 %fusion = bf16[4,40,7168]{2,1,0:T(8,128)(2,1)S(1)} fusion(f32[8,4,5,7168]{3,1,2,0:T(4,128)S(1)} %convert_reduce_fusion, f32[4,40,8]{1,2,0:T(8,128)S(1)} %bitcast_convert_fusion, s32[4,40,8]{1,2,0:T(8,128)S(1)} %bitcast.65), kind=kOutput, calls=%fused_computation.4 | convolution fusion | flops 551662080 | bytes 6891520 | tf_op jit(solution)/shard_map/nrgc,gncd->nrd/dot_general | solution.py:85
  461.3 32.6 %all_to_all.30 = bf16[4,40,7168]{2,1,0:T(8,128)(2,1)S(1)} all-to-all(bf16[4,40,7168]{2,1,0:T(8,128)(2,1)S(1)} %fusion), channel_id=1, replica_groups=mesh['node'=4,'local'=32] {'node'}, dimensions={0} | all-to-all | bytes 4587520 | tf_op jit(solution)/shard_map/all_to_all | solution.py:86
  493.9 1.9 fusion.1
  (34 shorter events, 5.6 us)
Async XLA Ops:
  0.0 7.9 %copy-start = (bf16[128,7168]{1,0:T(8,128)(2,1)S(1)}, bf16[128,7168]{1,0:T(8,128)(2,1)}, u32[]{:S(2)}) copy-start(bf16[128,7168]{1,0:T(8,128)(2,1)} %param.7) | copy-start | bytes 5505028
  3.4 9.8 %all-to-all-start = ((s32[4,1,320]{2,1,0:T(1,128)}), s32[4,1,320]{2,1,0:T(1,128)S(1)}, u32[]{:S(2)}, u32[]{:S(2)}) async-start(s32[4,1,320]{2,1,0:T(1,128)} %reshape.75), calls=%async_computation | async-start | bytes 12288 | tf_op jit(solution)/shard_map/all_to_all | solution.py:60
  13.2 31.8 %all-to-all-start.2 = ((bf16[4,40,7168]{2,1,0:T(8,128)(2,1)}), bf16[4,40,7168]{2,1,0:T(8,128)(2,1)}, u32[]{:S(2)}, u32[]{:S(2)}) async-start(bf16[4,40,7168]{2,1,0:T(8,128)(2,1)} %convolution_convert_fusion.2), calls=%async_computation.2 | async-start | bytes 4587520 | tf_op jit(solution)/shard_map/all_to_all | solution.py:58
  53.7 8.2 %copy-start.4 = (bf16[128,8]{0,1:T(8,128)(2,1)S(1)}, bf16[128,8]{0,1:T(8,128)(2,1)}, u32[]{:S(2)}) copy-start(bf16[128,8]{0,1:T(8,128)(2,1)} %param.9) | copy-start | bytes 6148
  53.7 8.2 %copy-start.3 = (s32[128,8]{0,1:T(8,128)S(1)}, s32[128,8]{0,1:T(8,128)}, u32[]{:S(2)}) copy-start(s32[128,8]{0,1:T(8,128)} %param.8) | copy-start | bytes 12292
  53.7 150.6 %all-to-all-start.3 = ((bf16[32,4,5,7168]{3,1,2,0:T(4,128)(2,1)}), bf16[32,4,5,7168]{3,1,2,0:T(4,128)(2,1)}, u32[]{:S(2)}, u32[]{:S(2)}) async-start(bf16[32,4,5,7168]{3,1,2,0:T(4,128)(2,1)} %bitcast.62), calls=%async_computation.3 | async-start | bytes 18350080 | tf_op jit(solution)/shard_map/all_to_all | solution.py:71
  204.2 93.2 %all-to-all-start.1 = ((bf16[4,2,160]{2,1,0:T(2,128)(2,1)}), bf16[4,2,160]{2,1,0:T(2,128)(2,1)S(1)}, u32[]{:S(2)}, u32[]{:S(2)}) async-start(bf16[4,2,160]{2,1,0:T(2,128)(2,1)} %reshape.77), calls=%async_computation.1 | async-start | bytes 8192 | tf_op jit(solution)/shard_map/all_to_all | solution.py:59
  236.4 12.1 %copy-start.2 = (bf16[640,7168]{1,0:T(8,128)(2,1)S(1)}, bf16[640,7168]{1,0:T(8,128)(2,1)}, u32[]{:S(2)}) copy-start(bf16[640,7168]{1,0:T(8,128)(2,1)} %reshape.65) | copy-start | bytes 27525124
  297.4 148.3 %all-to-all-start.4 = ((bf16[32,4,5,7168]{3,1,2,0:T(4,128)(2,1)}), bf16[32,4,5,7168]{3,1,2,0:T(4,128)(2,1)}, u32[]{:S(2)}, u32[]{:S(2)}) async-start(bf16[32,4,5,7168]{3,1,2,0:T(4,128)(2,1)} %copy.78), calls=%async_computation.4 | async-start | bytes 18350080 | tf_op jit(solution)/shard_map/all_to_all | solution.py:69
  455.1 40.8 %copy-start.1 = (bf16[128,7168]{1,0:T(8,128)(2,1)S(1)}, bf16[128,7168]{1,0:T(8,128)(2,1)}, u32[]{:S(2)}) copy-start(bf16[128,7168]{1,0:T(8,128)(2,1)} %param.7) | copy-start | bytes 5505028
where the time goes:
time: 498 us; the launch traced here: 496 us
  waiting for transfers between devices  313 us (63%)
  local copies, waits for them, and re-layouts  67.1 us (13%)
  matrix products  45.2 us (9%)
  blocking collectives  32.6 us (7%)
  starting transfers between devices  26.5 us (5%)
  other arithmetic  11.3 us (2%)
    all_to_all x1, waiting for transfers between devices, on_device(): lax.all_to_all(slab_output(lax.all_to_all(forward, 'local', split_axis=0,...  142 us
    all_to_all x1, waiting for transfers between devices, on_device(): lax.all_to_all(forward, 'local', split_axis=0, concat_axis=0, tiled=True)  141 us
    all_to_all x1, blocking collectives, on_device(): lax.all_to_all(merged.astype(jnp.bfloat16), 'node', split_axis=0, concat_...  32.6 us
    reshape x2, local copies, waits for them, and re-layouts, slab_output(): return result.reshape(packed.shape[:-1] + (down_slab.shape[1],))  28.8 us
    all_to_all x1, waiting for transfers between devices, on_device(): lax.all_to_all(rows_out, 'node', split_axis=0, concat_axis=0, tiled=True)  26.1 us
    reshape x1, local copies, waits for them, and re-layouts, slab_output(): flat_rows = packed.reshape(-1, packed.shape[-1])  15.1 us
    all_to_all x1, local copies, waits for them, and re-layouts, on_device(): lax.all_to_all(forward, 'local', split_axis=0, concat_axis=0, tiled=True)  13.7 us
    dot_general x1, matrix products, slab_output(): gate_act = jnp.dot(flat_rows, gate_slab, preferred_element_type=jnp.float32)  12.1 us
  transfers between devices with their start and end apart: 5, of which 4 were waited for; matrix products, arithmetic and copies ran while one was open for 19% of the time, Pallas kernels for 0%

commit v1 on v0

v1 whole, which is shorter than its diff:
```python
import functools

import jax
import jax.numpy as jnp
from jax import lax
from jax.experimental import pallas as pl
from jax.experimental.pallas import tpu as pltpu
from jax.sharding import PartitionSpec as P

GROUP = 4
CAP = 5
LANE_BLOCKS = 8
BUNDLE = 32
PIECE = 64
BF16 = jnp.bfloat16
F32 = jnp.float32


def shuffle_matrix(to_rows):
    size = BUNDLE * LANE_BLOCKS
    out = lax.broadcasted_iota(jnp.int32, (size, size), 0)
    src = lax.broadcasted_iota(jnp.int32, (size, size), 1)
    if to_rows:
        want = (out & (LANE_BLOCKS - 1)) * BUNDLE + (out >> 3)
    else:
        want = (out & (BUNDLE - 1)) * LANE_BLOCKS + (out >> 5)
    return (src == want).astype(BF16)


def unpack_rows(shuffle, packed, rows_ref, g):
    part = packed.shape[1]
    flat = jnp.dot(shuffle, packed, preferred_element_type=F32).astype(BF16)
    at = pl.multiple_of(g * BUNDLE, BUNDLE)
    for b in range(LANE_BLOCKS):
        rows_ref[pl.ds(at, BUNDLE), b * part : (b + 1) * part] = flat[b * BUNDLE : (b + 1) * BUNDLE]


def pack_rows(shuffle, rows_ref, g):
    part = rows_ref.shape[1] // LANE_BLOCKS
    at = pl.multiple_of(g * BUNDLE, BUNDLE)
    stacked = jnp.concatenate(
        [rows_ref[pl.ds(at, BUNDLE), b * part : (b + 1) * part] for b in range(LANE_BLOCKS)], axis=0
    )
    return jnp.dot(shuffle, stacked, preferred_element_type=F32).astype(BF16)


def dispatch_kernel(limits_ref, ids_ref, gates_ref, tokens_ref, send_ref, coef_ref, rows_ref):
    toks = tokens_ref.shape[0]
    slots = rows_ref.shape[0]
    experts = slots // (2 * CAP)
    expert_at = lax.broadcasted_iota(jnp.int32, (experts, toks), 0)
    named = jnp.zeros((experts, toks), F32)
    gate = jnp.zeros((experts, toks), F32)
    for k in range(ids_ref.shape[0]):
        hit = ids_ref[k : k + 1, :] == expert_at
        named = named + jnp.where(hit, 1.0, 0.0)
        gate = gate + jnp.where(hit, gates_ref[k : k + 1, :].astype(F32), 0.0)
    earlier = (
        lax.broadcasted_iota(jnp.int32, (toks, toks), 0) < lax.broadcasted_iota(jnp.int32, (toks, toks), 1)
    ).astype(BF16)
    before = jnp.dot(named.astype(BF16), earlier, preferred_element_type=F32)
    capacity = jnp.zeros((experts, toks), F32)
    for e in range(experts):
        capacity = jnp.where(expert_at == e, limits_ref[e].astype(F32), capacity)
    kept = (named > 0) & (before < capacity)
    rank = jnp.where(kept, before + 1.0, 0.0)
    slot = lax.broadcasted_iota(jnp.int32, (slots, experts), 0)
    first = lax.broadcasted_iota(jnp.int32, (slots, experts), 1) * (2 * CAP)
    spread = ((slot >= first) & (slot < first + 2 * CAP)).astype(BF16)
    slot_rank = jnp.dot(spread, rank.astype(BF16), preferred_element_type=F32)
    slot_gate = jnp.dot(spread, gate.astype(BF16), preferred_element_type=F32)
    place = lax.rem(lax.broadcasted_iota(jnp.int32, (slots, toks), 0), CAP).astype(F32) + 1.0
    taken = slot_rank == place
    coef_ref[...] = jnp.where(taken, slot_gate, 0.0).T.astype(BF16)
    pick = jnp.where(taken, 1.0, 0.0).astype(BF16)
    width = tokens_ref.shape[1]
    step = 512

    @pl.loop(0, width // step)
    def _(j):
        at = pl.ds(pl.multiple_of(j * step, step), step)
        rows_ref[:, at] = jnp.dot(pick, tokens_ref[:, at], preferred_element_type=F32).astype(BF16)

    shuffle = shuffle_matrix(True)
    size = BUNDLE * LANE_BLOCKS

    @pl.loop(0, slots // BUNDLE)
    def _(g):
        send_ref[pl.ds(pl.multiple_of(g * size, size), size), :] = pack_rows(shuffle, rows_ref, g)


def experts_kernel(
    x_hbm, g0, g1, u0, u1, d0, d1, y_hbm, x_buf, rows_ref, w_buf, d_buf, acc_ref, x_sem, w_sem, d_sem, y_sem
):
    rows, width = rows_ref.shape
    slab = g0.shape[0]
    size = BUNDLE * LANE_BLOCKS
    bundles = rows // BUNDLE
    n_tile = 256
    per_tile = n_tile // PIECE
    tiles = 4 * slab // n_tile
    per_slab = slab // PIECE
    d_step = 512
    d_steps = width // d_step

    def x_copy(g):
        at = pl.ds(pl.multiple_of(g * size, size), size)
        return pltpu.make_async_copy(x_hbm.at[at, :], x_buf.at[at, :], x_sem.at[g])

    def y_copy(g):
        at = pl.ds(pl.multiple_of(g * size, size), size)
        return pltpu.make_async_copy(x_buf.at[at, :], y_hbm.at[at, :], y_sem.at[g])

    def w_copies(tile):
        copies = []
        for piece in range(tile * per_tile, (tile + 1) * per_tile):
            source = (g0, g1, u0, u1)[piece // per_slab]
            at = (piece % per_slab) * PIECE
            copies.append(
                pltpu.make_async_copy(
                    source.at[pl.ds(at, PIECE), :], w_buf.at[pl.ds(piece * PIECE, PIECE), :], w_sem.at[piece]
                )
            )
        return copies

    def d_copies(step):
        at = pl.ds(step * d_step, d_step)
        return [
            pltpu.make_async_copy(d.at[:, at], d_buf.at[pl.ds(i * slab, slab), at], d_sem.at[step, i])
            for i, d in enumerate((d0, d1))
        ]

    queue = [w_copies(i) for i in range(tiles)] + [d_copies(i) for i in range(d_steps)]
    ahead = 3

    def start(i):
        if i < len(queue):
            for copy in queue[i]:
                copy.start()

    for g in range(bundles):
        x_copy(g).start()
    for i in range(ahead):
        start(i)
    shuffle = shuffle_matrix(False)

    @pl.loop(0, bundles)
    def _(g):
        x_copy(g).wait()
        at = pl.ds(pl.multiple_of(g * size, size), size)
        unpack_rows(shuffle, x_buf[at, :], rows_ref, g)

    for tile in range(tiles):
        for copy in queue[tile]:
            copy.wait()
        start(tile + ahead)
        acc_ref[:, tile * n_tile : (tile + 1) * n_tile] = lax.dot_general(
            rows_ref[...],
            w_buf[tile * n_tile : (tile + 1) * n_tile, :],
            (((1,), (1,)), ((), ())),
            preferred_element_type=F32,
        )
    gate = acc_ref[:, : 2 * slab]
    hidden = (gate / (1.0 + jnp.exp(-gate)) * acc_ref[:, 2 * slab :]).astype(BF16)
    for step in range(d_steps):
        for copy in queue[tiles + step]:
            copy.wait()
        start(tiles + step + ahead)
        at = slice(step * d_step, (step + 1) * d_step)
        rows_ref[:, at] = jnp.dot(hidden, d_buf[:, at], preferred_element_type=F32).astype(BF16)
    back = shuffle_matrix(True)

    @pl.loop(0, bundles)
    def _(g):
        at = pl.ds(pl.multiple_of(g * size, size), size)
        x_buf[at, :] = pack_rows(back, rows_ref, g)
        y_copy(g).start()

    @pl.loop(0, bundles)
    def _(g):
        y_copy(g).wait()


def combine_kernel(coef_ref, y_ref, out_ref, rows_ref):
    size = BUNDLE * LANE_BLOCKS
    shuffle = shuffle_matrix(False)

    @pl.loop(0, rows_ref.shape[0] // BUNDLE)
    def _(g):
        at = pl.ds(pl.multiple_of(g * size, size), size)
        unpack_rows(shuffle, y_ref[at, :], rows_ref, g)

    step = 512

    @pl.loop(0, out_ref.shape[1] // step)
    def _(j):
        at = pl.ds(pl.multiple_of(j * step, step), step)
        out_ref[:, at] = jnp.dot(coef_ref[...], rows_ref[:, at], preferred_element_type=F32).astype(BF16)


def on_device(tokens, route_ids, route_gates, limits, w_gate, w_up, w_down):
    axes = ("node", "local")
    devices = lax.axis_size("node") * lax.axis_size("local")
    chips = devices // 2
    toks, width = tokens.shape
    slab = w_gate.shape[2]
    slots = chips * CAP
    part = width // LANE_BLOCKS
    vmem = pl.BlockSpec(memory_space=pltpu.VMEM)
    smem = pl.BlockSpec(memory_space=pltpu.SMEM)
    anywhere = pl.BlockSpec(memory_space=pl.ANY)
    limit = pltpu.CompilerParams(vmem_limit_bytes=60 * 1024 * 1024)

    gate_slab, up_slab, down_slab = w_gate[0].T, w_up[0].T, w_down[0]
    swap = [(i, i ^ 1) for i in range(devices)]
    with jax.named_scope("sibling_weights"):
        gate_other = lax.ppermute(gate_slab, axes, swap)
        up_other = lax.ppermute(up_slab, axes, swap)
        down_other = lax.ppermute(down_slab, axes, swap)

    send, coef = pl.pallas_call(
        dispatch_kernel,
        out_shape=(
            jax.ShapeDtypeStruct((slots * LANE_BLOCKS, part), BF16),
            jax.ShapeDtypeStruct((toks, slots), BF16),
        ),
        in_specs=[smem, vmem, vmem, vmem],
        out_specs=(vmem, vmem),
        scratch_shapes=[pltpu.VMEM((slots, width), BF16)],
        compiler_params=limit,
        name="dispatch",
    )(limits, route_ids.T, route_gates.T, tokens)

    same_core = [[2 * k + c for k in range(chips)] for c in range(2)]

    def exchange(rows):
        rows = rows.reshape(chips, CAP * LANE_BLOCKS, part)
        rows = lax.all_to_all(rows, axes, 0, 0, axis_index_groups=same_core, tiled=True)
        return rows.reshape(slots * LANE_BLOCKS, part)

    received = exchange(send)
    pieces = 4 * slab // PIECE
    bundles = slots // BUNDLE
    partial = pl.pallas_call(
        experts_kernel,
        out_shape=jax.ShapeDtypeStruct((slots * LANE_BLOCKS, part), BF16),
        in_specs=[anywhere] * 7,
        out_specs=anywhere,
        scratch_shapes=[
            pltpu.VMEM((slots * LANE_BLOCKS, part), BF16),
            pltpu.VMEM((slots, width), BF16),
            pltpu.VMEM((4 * slab, width), BF16),
            pltpu.VMEM((2 * slab, width), BF16),
            pltpu.VMEM((slots, 4 * slab), F32),
            pltpu.SemaphoreType.DMA((bundles,)),
            pltpu.SemaphoreType.DMA((pieces,)),
            pltpu.SemaphoreType.DMA((width // 512, 2)),
            pltpu.SemaphoreType.DMA((bundles,)),
        ],
        compiler_params=limit,
        name="experts",
    )(received, gate_slab, gate_other, up_slab, up_other, down_slab, down_other)

    returned = exchange(partial)
    return pl.pallas_call(
        combine_kernel,
        out_shape=jax.ShapeDtypeStruct((toks, width), BF16),
        in_specs=[vmem, vmem],
        out_specs=vmem,
        scratch_shapes=[pltpu.VMEM((slots, width), BF16)],
        compiler_params=limit,
        name="combine",
    )(coef, returned)


def solution(mesh):
    return jax.shard_map(
        on_device,
        mesh=mesh,
        in_specs=(
            P(("node", "local"), None),
            P(("node", "local"), None),
            P(("node", "local"), None),
            P(),
            P(("node", "local"), None, None),
            P(("node", "local"), None, None),
            P(("node", "local"), None, None),
        ),
        out_specs=P(("node", "local"), None),
        check_vma=False,
    )
```

time: 498 us -> 189 us (0.38)
  the two profiles are of different devices: /device:TPU:36 before, /device:TPU:0 now
where the time goes in v1:
time: 189 us
  blocking collectives  132 us (70%)
  Pallas kernels  56.9 us (30%)
    all_to_all x2, blocking collectives, exchange(): lax.all_to_all(rows, axes, 0, 0, axis_index_groups=same_core, tiled=True)  132 us
    pallas_call x1, Pallas kernels, on_device(): pl.pallas_call(experts_kernel, out_shape=jax.ShapeDtypeStruct((slots * LA...  36.5 us
    pallas_call x1, Pallas kernels, on_device(): pl.pallas_call(dispatch_kernel, out_shape=(jax.ShapeDtypeStruct((slots *...  10.5 us
    pallas_call x1, Pallas kernels, on_device(): pl.pallas_call(combine_kernel, out_shape=jax.ShapeDtypeStruct((toks, widt...  9.93 us
  transfers between devices with their start and end apart: 3, of which 0 were waited for; matrix products, arithmetic and copies ran while one was open for 0% of the time, Pallas kernels for 6%

profile of v1, /device:TPU:0, one launch (start us, length us, event | category | flops | bytes accessed | tf_op | source)
XLA Modules:
  0.0 189.2 jit_solution(13794744752950471193)
XLA Ops:
  0.0 0.0 collective-permute-start
  0.0 0.5 collective-permute-start.1
  0.5 0.0 collective-permute-start.2
  0.5 10.5 %dispatch.1 = (bf16[2560,896]{1,0:T(8,128)(2,1)}, bf16[128,320]{1,0:T(8,128)(2,1)}) custom-call(s32[384]{0:T(512)} %limits_ref.1, s32[8,128]{1,0:T(8,128)} %bitcast.23, bf16[8,128]{1,0:T(8,128)(2,1)} %bitcast.24, bf16[128,7168]{1,0:T(8,128)(2,1)} %tokens_ref.1), custom_call_target="tpu_custom_call" | custom-call | tf_op jit(solution)/shard_map/dispatch/pallas_call | solution.py:221
  11.1 69.1 %all_to_all.10 = bf16[64,40,896]{2,1,0:T(8,128)(2,1)} all-to-all(bf16[64,40,896]{2,1,0:T(8,128)(2,1)} %bitcast.22), channel_id=1, replica_groups={{0,2,4,6,8,10,12,14,16,18,20,22,24,26,28,30,32,34,36,38,40,42,44,46,48,..., dimensions={0} | all-to-all | bytes 9175040 | tf_op jit(solution)/shard_map/all_to_all | solution.py:238
  80.2 0.0 collective-permute-done.g1
  80.2 0.0 collective-permute-done.1.u1
  80.2 0.0 collective-permute-done.2.d1
  80.2 36.5 %experts.1 = bf16[2560,896]{1,0:T(8,128)(2,1)} custom-call(bf16[2560,896]{1,0:T(8,128)(2,1)} %bitcast.13, bf16[448,7168]{1,0:T(8,128)(2,1)} %bitcast.17, bf16[448,7168]{1,0:T(8,128)(2,1)} %collective-permute-done.g1, bf16[448,7168]{1,0:T(8,128)(2,1)} %bitcast.19, bf16[448,7168]{1,0:T(8,128)(2,1)} %collective-permute-done.1.u1, bf16[448,7168]{1,0:T(8,128)(2,1)} %bitcast.21, ...), custom_call_target="tpu_custom_call" | custom-call | tf_op jit(solution)/shard_map/experts/pallas_call | solution.py:244
  116.7 62.6 %all_to_all.11 = bf16[64,40,896]{2,1,0:T(8,128)(2,1)} all-to-all(bf16[64,40,896]{2,1,0:T(8,128)(2,1)} %bitcast.14), channel_id=1, replica_groups={{0,2,4,6,8,10,12,14,16,18,20,22,24,26,28,30,32,34,36,38,40,42,44,46,48,..., dimensions={0} | all-to-all | bytes 9175040 | tf_op jit(solution)/shard_map/all_to_all | solution.py:238
  179.2 9.9 %combine.1 = bf16[128,7168]{1,0:T(8,128)(2,1)} custom-call(bf16[128,320]{1,0:T(8,128)(2,1)} %get-tuple-element.7.coef_ref, bf16[2560,896]{1,0:T(8,128)(2,1)} %bitcast.15), custom_call_target="tpu_custom_call" | custom-call | tf_op jit(solution)/shard_map/combine/pallas_call | solution.py:265
Async XLA Ops:
  0.0 80.2 %collective-permute-start = (bf16[448,7168]{1,0:T(8,128)(2,1)}, bf16[448,7168]{1,0:T(8,128)(2,1)}, u32[]{:S(2)}, u32[]{:S(2)}) collective-permute-start(bf16[448,7168]{1,0:T(8,128)(2,1)} %bitcast.16), channel_id=1, source_target_pairs={{0,1},{1,0},{2,3},{3,2},{4,5},{5,4},{6,7},{7,6},{8,9},{9,8},{10,11... | collective-permute-start | bytes 19267592 | tf_op jit(solution)/shard_map/sibling_weights/ppermute | solution.py:217
  0.0 80.2 %collective-permute-start.1 = (bf16[448,7168]{1,0:T(8,128)(2,1)}, bf16[448,7168]{1,0:T(8,128)(2,1)}, u32[]{:S(2)}, u32[]{:S(2)}) collective-permute-start(bf16[448,7168]{1,0:T(8,128)(2,1)} %bitcast.18), channel_id=1, source_target_pairs={{0,1},{1,0},{2,3},{3,2},{4,5},{5,4},{6,7},{7,6},{8,9},{9,8},{10,11... | collective-permute-start | bytes 19267592 | tf_op jit(solution)/shard_map/sibling_weights/ppermute | solution.py:218
  0.5 79.7 %collective-permute-start.2 = (bf16[448,7168]{1,0:T(8,128)(2,1)}, bf16[448,7168]{1,0:T(8,128)(2,1)}, u32[]{:S(2)}, u32[]{:S(2)}) collective-permute-start(bf16[448,7168]{1,0:T(8,128)(2,1)} %bitcast.20), channel_id=1, source_target_pairs={{0,1},{1,0},{2,3},{3,2},{4,5},{5,4},{6,7},{7,6},{8,9},{9,8},{10,11... | collective-permute-start | bytes 19267592 | tf_op jit(solution)/shard_map/sibling_weights/ppermute | solution.py:219

commit v2 on v1

v2 whole, which is shorter than its diff:
```python
import jax
import jax.numpy as jnp
from jax import lax
from jax.experimental import pallas as pl
from jax.experimental.pallas import tpu as pltpu
from jax.sharding import PartitionSpec as P

GROUP = 4
CAP = 5
LANE_BLOCKS = 8
BUNDLE = 32
MIB = 1024 * 1024
BF16 = jnp.bfloat16
F32 = jnp.float32


def in_vmem(array):
    return pltpu.with_memory_space_constraint(array, pltpu.VMEM)


def in_hbm(array):
    return pltpu.with_memory_space_constraint(array, pltpu.HBM)


def shuffle_matrix(to_rows):
    size = BUNDLE * LANE_BLOCKS
    out = lax.broadcasted_iota(jnp.int32, (size, size), 0)
    src = lax.broadcasted_iota(jnp.int32, (size, size), 1)
    if to_rows:
        want = (out & (LANE_BLOCKS - 1)) * BUNDLE + (out >> 3)
    else:
        want = (out & (BUNDLE - 1)) * LANE_BLOCKS + (out >> 5)
    return (src == want).astype(BF16)


def unpack_rows(shuffle, packed, rows_ref, g):
    part = packed.shape[1]
    flat = jnp.dot(shuffle, packed, preferred_element_type=F32).astype(BF16)
    at = g * BUNDLE
    for b in range(LANE_BLOCKS):
        rows_ref[at : at + BUNDLE, b * part : (b + 1) * part] = flat[b * BUNDLE : (b + 1) * BUNDLE]


def pack_rows(shuffle, rows_ref, g):
    part = rows_ref.shape[1] // LANE_BLOCKS
    at = g * BUNDLE
    stacked = jnp.concatenate(
        [rows_ref[at : at + BUNDLE, b * part : (b + 1) * part] for b in range(LANE_BLOCKS)], axis=0
    )
    return jnp.dot(shuffle, stacked, preferred_element_type=F32).astype(BF16)


def dispatch_kernel(
    limits_ref, ids_ref, gates_ref, tokens_hbm, send_ref, coef_ref, tokens_ref, rows_ref, tokens_sem
):
    fetch = pltpu.make_async_copy(tokens_hbm, tokens_ref, tokens_sem)
    fetch.start()
    toks, width = tokens_ref.shape
    slots = rows_ref.shape[0]
    experts = slots // CAP
    expert_at = lax.broadcasted_iota(jnp.int32, (experts, toks), 0)
    named = jnp.zeros((experts, toks), F32)
    gate = jnp.zeros((experts, toks), F32)
    for k in range(ids_ref.shape[0]):
        hit = ids_ref[k : k + 1, :] == expert_at
        named = named + jnp.where(hit, 1.0, 0.0)
        gate = gate + jnp.where(hit, gates_ref[k : k + 1, :].astype(F32), 0.0)
    earlier = (
        lax.broadcasted_iota(jnp.int32, (toks, toks), 0) < lax.broadcasted_iota(jnp.int32, (toks, toks), 1)
    ).astype(BF16)
    before = jnp.dot(named.astype(BF16), earlier, preferred_element_type=F32)
    capacity = jnp.zeros((experts, toks), F32)
    for e in range(experts):
        capacity = jnp.where(expert_at == e, limits_ref[e].astype(F32), capacity)
    kept = (named > 0) & (before < capacity)
    rank = jnp.where(kept, before + 1.0, 0.0)
    slot = lax.broadcasted_iota(jnp.int32, (slots, experts), 0)
    first = lax.broadcasted_iota(jnp.int32, (slots, experts), 1) * CAP
    spread = ((slot >= first) & (slot < first + CAP)).astype(BF16)
    slot_rank = jnp.dot(spread, rank.astype(BF16), preferred_element_type=F32)
    slot_gate = jnp.dot(spread, gate.astype(BF16), preferred_element_type=F32)
    place = lax.rem(lax.broadcasted_iota(jnp.int32, (slots, toks), 0), CAP).astype(F32) + 1.0
    taken = slot_rank == place
    pick = jnp.where(taken, 1.0, 0.0).astype(BF16)
    fetch.wait()
    step = 1024
    for at in range(0, width, step):
        rows_ref[:, at : at + step] = jnp.dot(
            pick, tokens_ref[:, at : at + step], preferred_element_type=F32
        ).astype(BF16)
    shuffle = shuffle_matrix(True)
    size = BUNDLE * LANE_BLOCKS
    for g in range(slots // BUNDLE):
        packed = pack_rows(shuffle, rows_ref, g)
        for h in range(2):
            send_ref[h, g * size : (g + 1) * size, :] = packed
    coef_ref[...] = jnp.where(taken, slot_gate, 0.0).T.astype(BF16)


def experts_kernel(
    x_ref, g1, u1, d1, g0_hbm, u0_hbm, d0_hbm, y_ref, g0, u0, d0, rows_ref, hidden_ref, sem
):
    fetches = [
        pltpu.make_async_copy(source, place, sem.at[i])
        for i, (source, place) in enumerate(((g0_hbm, g0), (u0_hbm, u0), (d0_hbm, d0)))
    ]
    for fetch in fetches:
        fetch.start()
    rows, width = rows_ref.shape
    size = BUNDLE * LANE_BLOCKS
    bundles = rows // BUNDLE
    shuffle = shuffle_matrix(False)
    for g in range(bundles):
        unpack_rows(shuffle, x_ref[g * size : (g + 1) * size, :], rows_ref, g)
    across = (((1,), (1,)), ((), ()))

    def slab_hidden(gate_w, up_w):
        gate = lax.dot_general(rows_ref[...], gate_w[...], across, preferred_element_type=F32)
        upper = lax.dot_general(rows_ref[...], up_w[...], across, preferred_element_type=F32)
        return (gate / (1.0 + jnp.exp(-gate)) * upper).astype(BF16)

    hidden_ref[1] = slab_hidden(g1, u1)
    fetches[0].wait()
    fetches[1].wait()
    hidden_ref[0] = slab_hidden(g0, u0)
    fetches[2].wait()
    step = 1024
    for at in range(0, width, step):
        total = jnp.dot(hidden_ref[0], d0[:, at : at + step], preferred_element_type=F32)
        total += jnp.dot(hidden_ref[1], d1[:, at : at + step], preferred_element_type=F32)
        rows_ref[:, at : at + step] = total.astype(BF16)
    back = shuffle_matrix(True)
    for g in range(bundles):
        y_ref[g * size : (g + 1) * size, :] = pack_rows(back, rows_ref, g)


def combine_kernel(coef_ref, y_ref, out_hbm, out_ref, rows_ref, sem):
    size = BUNDLE * LANE_BLOCKS
    shuffle = shuffle_matrix(False)
    for g in range(rows_ref.shape[0] // BUNDLE):
        unpack_rows(shuffle, y_ref[g * size : (g + 1) * size, :], rows_ref, g)
    half = rows_ref.shape[0] // 2
    step = 1024
    copies = []
    for i, at in enumerate(range(0, out_ref.shape[1], step)):
        total = jnp.dot(coef_ref[...], rows_ref[:half, at : at + step], preferred_element_type=F32)
        total += jnp.dot(coef_ref[...], rows_ref[half:, at : at + step], preferred_element_type=F32)
        out_ref[:, at : at + step] = total.astype(BF16)
        columns = pl.ds(at, step)
        copies.append(pltpu.make_async_copy(out_ref.at[:, columns], out_hbm.at[:, columns], sem.at[i]))
        copies[-1].start()
    for copy in copies:
        copy.wait()


def on_device(tokens, route_ids, route_gates, limits, w_gate, w_up, w_down):
    axes = ("node", "local")
    devices = lax.axis_size("node") * lax.axis_size("local")
    chips = devices // 2
    hosted = chips // 2
    toks, width = tokens.shape
    slab = w_gate.shape[2]
    slots = hosted * CAP
    part = width // LANE_BLOCKS
    vmem = pl.BlockSpec(memory_space=pltpu.VMEM)
    smem = pl.BlockSpec(memory_space=pltpu.SMEM)
    anywhere = pl.BlockSpec(memory_space=pl.ANY)

    gate_slab, up_slab, down_slab = w_gate[0].T, w_up[0].T, w_down[0]
    swap = [(i, i ^ 1) for i in range(devices)]
    with jax.named_scope("sibling_weights"):
        gate_other = lax.ppermute(gate_slab, axes, swap)
        up_other = lax.ppermute(up_slab, axes, swap)
        down_other = lax.ppermute(down_slab, axes, swap)

    send, coef = pl.pallas_call(
        dispatch_kernel,
        out_shape=(
            pltpu.VMEM((2, slots * LANE_BLOCKS, part), BF16),
            pltpu.VMEM((toks, slots), BF16),
        ),
        in_specs=[smem, vmem, vmem, anywhere],
        out_specs=(vmem, vmem),
        scratch_shapes=[
            pltpu.VMEM((toks, width), BF16),
            pltpu.VMEM((slots, width), BF16),
            pltpu.SemaphoreType.DMA,
        ],
        compiler_params=pltpu.CompilerParams(vmem_limit_bytes=8 * MIB),
        name="dispatch",
    )(in_hbm(limits), in_hbm(route_ids.T), in_hbm(route_gates.T), in_hbm(tokens))

    order = [2 * (2 * e + h) for h in range(2) for e in range(hosted)]
    same_core = [[i + c for i in order] for c in range(2)]

    def exchange(rows):
        rows = rows.reshape(chips, CAP * LANE_BLOCKS, part)
        rows = lax.all_to_all(rows, axes, 0, 0, axis_index_groups=same_core, tiled=True)
        return rows.reshape(2 * slots * LANE_BLOCKS, part)

    received = exchange(send)
    slab_shapes = [pltpu.VMEM(w.shape, BF16) for w in (gate_slab, up_slab, down_slab)]
    partial = pl.pallas_call(
        experts_kernel,
        out_shape=pltpu.VMEM((2 * slots * LANE_BLOCKS, part), BF16),
        in_specs=[vmem] * 4 + [anywhere] * 3,
        out_specs=vmem,
        scratch_shapes=slab_shapes
        + [
            pltpu.VMEM((2 * slots, width), BF16),
            pltpu.VMEM((2, 2 * slots, slab), BF16),
            pltpu.SemaphoreType.DMA((3,)),
        ],
        compiler_params=pltpu.CompilerParams(vmem_limit_bytes=30 * MIB),
        name="experts",
    )(
        in_vmem(received),
        in_vmem(gate_other),
        in_vmem(up_other),
        in_vmem(down_other),
        in_hbm(gate_slab),
        in_hbm(up_slab),
        in_hbm(down_slab),
    )

    returned = exchange(partial)
    return pl.pallas_call(
        combine_kernel,
        out_shape=jax.ShapeDtypeStruct((toks, width), BF16),
        in_specs=[vmem, vmem],
        out_specs=anywhere,
        scratch_shapes=[
            pltpu.VMEM((toks, width), BF16),
            pltpu.VMEM((2 * slots, width), BF16),
            pltpu.SemaphoreType.DMA((width // 1024,)),
        ],
        compiler_params=pltpu.CompilerParams(vmem_limit_bytes=12 * MIB),
        name="combine",
    )(in_vmem(coef), in_vmem(returned))


def solution(mesh):
    return jax.shard_map(
        on_device,
        mesh=mesh,
        in_specs=(
            P(("node", "local"), None),
            P(("node", "local"), None),
            P(("node", "local"), None),
            P(),
            P(("node", "local"), None, None),
            P(("node", "local"), None, None),
            P(("node", "local"), None, None),
        ),
        out_specs=P(("node", "local"), None),
        check_vma=False,
    )
```

time: 189 us -> 160 us (0.85)
  Pallas kernels: 56.9 us -> 29.4 us
  blocking collectives: 132 us -> 130 us
    pallas_call x2, Pallas kernels: 47 us -> 26 us  [the longest x1 22.2 us: on_device(): pl.pallas_call(experts_kernel, out_shape=pltpu.VMEM((2 * slots * LANE_BLO...]
    pallas_call x1, Pallas kernels: 9.93 us -> 3.32 us  [on_device(): pl.pallas_call(combine_kernel, out_shape=jax.ShapeDtypeStruct((toks, widt...]
  transfers between devices with their start and end apart: 3 -> 3, of which waited for: 0 -> 0; matrix products, arithmetic and copies ran while one was open for 0% -> 0% of each run, Pallas kernels for 6% -> 2%
where the time goes in v2:
time: 160 us
  blocking collectives  130 us (81%)
  Pallas kernels  29.4 us (18%)
    all_to_all x2, blocking collectives, exchange(): lax.all_to_all(rows, axes, 0, 0, axis_index_groups=same_core, tiled=True)  130 us
    pallas_call x1, Pallas kernels, on_device(): pl.pallas_call(experts_kernel, out_shape=pltpu.VMEM((2 * slots * LANE_BLO...  22.2 us
    pallas_call x1, Pallas kernels, on_device(): pl.pallas_call(dispatch_kernel, out_shape=(pltpu.VMEM((2, slots * LANE_BL...  3.8 us
    pallas_call x1, Pallas kernels, on_device(): pl.pallas_call(combine_kernel, out_shape=jax.ShapeDtypeStruct((toks, widt...  3.32 us
  transfers between devices with their start and end apart: 3, of which 0 were waited for; matrix products, arithmetic and copies ran while one was open for 0% of the time, Pallas kernels for 2%

profile of v2, /device:TPU:0, one launch (start us, length us, event | category | flops | bytes accessed | tf_op | source)
XLA Modules:
  0.0 159.9 jit_solution(14320151100127051397)
XLA Ops:
  0.0 0.0 collective-permute-start
  0.0 0.5 collective-permute-start.1
  0.5 0.0 collective-permute-start.2
  0.5 3.8 %dispatch.1 = (bf16[2,1280,896]{2,1,0:T(8,128)(2,1)S(1)}, bf16[128,160]{1,0:T(8,128)(2,1)S(1)}) custom-call(s32[384]{0:T(512)} %limits_ref.1, s32[8,128]{1,0:T(8,128)} %bitcast.23, bf16[8,128]{1,0:T(8,128)(2,1)} %bitcast.24, bf16[128,7168]{1,0:T(8,128)(2,1)} %tokens_hbm.1), custom_call_target="tpu_custom_call" | custom-call | tf_op jit(solution)/shard_map/dispatch/pallas_call | solution.py:176
  4.3 68.7 %all_to_all.10 = bf16[64,40,896]{2,1,0:T(8,128)(2,1)S(1)} all-to-all(bf16[64,40,896]{2,1,0:T(8,128)(2,1)S(1)} %bitcast.16), channel_id=1, replica_groups={{0,4,8,12,16,20,24,28,32,36,40,44,48,52,56,60,64,68,72,76,80,84,88,92,9..., dimensions={0} | all-to-all | bytes 9175040 | tf_op jit(solution)/shard_map/all_to_all | solution.py:198
  73.1 0.0 collective-permute-done.g1
  73.1 0.0 collective-permute-done.1.u1
  73.1 0.0 collective-permute-done.2.d1
  73.1 22.2 %experts.1 = bf16[2560,896]{1,0:T(8,128)(2,1)S(1)} custom-call(bf16[2560,896]{1,0:T(8,128)(2,1)S(1)} %bitcast.13, bf16[448,7168]{1,0:T(8,128)(2,1)S(1)} %collective-permute-done.g1, bf16[448,7168]{1,0:T(8,128)(2,1)S(1)} %collective-permute-done.1.u1, bf16[448,7168]{1,0:T(8,128)(2,1)S(1)} %collective-permute-done.2.d1, bf16[448,7168]{1,0:T(8,128)(2,1)} %bitcast.18, ...), custom_call_target="tpu_custom_call" | custom-call | tf_op jit(solution)/shard_map/experts/pallas_call | solution.py:203
  95.3 61.1 %all_to_all.11 = bf16[64,40,896]{2,1,0:T(8,128)(2,1)S(1)} all-to-all(bf16[64,40,896]{2,1,0:T(8,128)(2,1)S(1)} %bitcast.14), channel_id=1, replica_groups={{0,4,8,12,16,20,24,28,32,36,40,44,48,52,56,60,64,68,72,76,80,84,88,92,9..., dimensions={0} | all-to-all | bytes 9175040 | tf_op jit(solution)/shard_map/all_to_all | solution.py:198
  156.4 3.3 %combine.1 = bf16[128,7168]{1,0:T(8,128)(2,1)} custom-call(bf16[128,160]{1,0:T(8,128)(2,1)S(1)} %get-tuple-element.7.coef_ref, bf16[2560,896]{1,0:T(8,128)(2,1)S(1)} %bitcast.15), custom_call_target="tpu_custom_call" | custom-call | tf_op jit(solution)/shard_map/combine/pallas_call | solution.py:227
Async XLA Ops:
  0.0 73.1 %collective-permute-start = (bf16[448,7168]{1,0:T(8,128)(2,1)}, bf16[448,7168]{1,0:T(8,128)(2,1)S(1)}, u32[]{:S(2)}, u32[]{:S(2)}) collective-permute-start(bf16[448,7168]{1,0:T(8,128)(2,1)} %bitcast.17), channel_id=1, source_target_pairs={{0,1},{1,0},{2,3},{3,2},{4,5},{5,4},{6,7},{7,6},{8,9},{9,8},{10,11... | collective-permute-start | bytes 19267592 | tf_op jit(solution)/shard_map/sibling_weights/ppermute | solution.py:172
  0.0 73.1 %collective-permute-start.1 = (bf16[448,7168]{1,0:T(8,128)(2,1)}, bf16[448,7168]{1,0:T(8,128)(2,1)S(1)}, u32[]{:S(2)}, u32[]{:S(2)}) collective-permute-start(bf16[448,7168]{1,0:T(8,128)(2,1)} %bitcast.19), channel_id=1, source_target_pairs={{0,1},{1,0},{2,3},{3,2},{4,5},{5,4},{6,7},{7,6},{8,9},{9,8},{10,11... | collective-permute-start | bytes 19267592 | tf_op jit(solution)/shard_map/sibling_weights/ppermute | solution.py:173
  0.5 72.6 %collective-permute-start.2 = (bf16[448,7168]{1,0:T(8,128)(2,1)}, bf16[448,7168]{1,0:T(8,128)(2,1)S(1)}, u32[]{:S(2)}, u32[]{:S(2)}) collective-permute-start(bf16[448,7168]{1,0:T(8,128)(2,1)} %bitcast.21), channel_id=1, source_target_pairs={{0,1},{1,0},{2,3},{3,2},{4,5},{5,4},{6,7},{7,6},{8,9},{9,8},{10,11... | collective-permute-start | bytes 19267592 | tf_op jit(solution)/shard_map/sibling_weights/ppermute | solution.py:174

commit v3 on v2

--- a/solution.py
+++ b/solution.py
@@ -97,15 +97,7 @@
     coef_ref[...] = jnp.where(taken, slot_gate, 0.0).T.astype(BF16)
 
 
-def experts_kernel(
-    x_ref, g1, u1, d1, g0_hbm, u0_hbm, d0_hbm, y_ref, g0, u0, d0, rows_ref, hidden_ref, sem
-):
-    fetches = [
-        pltpu.make_async_copy(source, place, sem.at[i])
-        for i, (source, place) in enumerate(((g0_hbm, g0), (u0_hbm, u0), (d0_hbm, d0)))
-    ]
-    for fetch in fetches:
-        fetch.start()
+def experts_kernel(x_ref, g0, u0, d0, g1, u1, d1, y_ref, rows_ref, hidden_ref):
     rows, width = rows_ref.shape
     size = BUNDLE * LANE_BLOCKS
     bundles = rows // BUNDLE
@@ -119,11 +111,8 @@
         upper = lax.dot_general(rows_ref[...], up_w[...], across, preferred_element_type=F32)
         return (gate / (1.0 + jnp.exp(-gate)) * upper).astype(BF16)
 
+    hidden_ref[0] = slab_hidden(g0, u0)
     hidden_ref[1] = slab_hidden(g1, u1)
-    fetches[0].wait()
-    fetches[1].wait()
-    hidden_ref[0] = slab_hidden(g0, u0)
-    fetches[2].wait()
     step = 1024
     for at in range(0, width, step):
         total = jnp.dot(hidden_ref[0], d0[:, at : at + step], preferred_element_type=F32)
@@ -172,6 +161,9 @@
         gate_other = lax.ppermute(gate_slab, axes, swap)
         up_other = lax.ppermute(up_slab, axes, swap)
         down_other = lax.ppermute(down_slab, axes, swap)
+        stay = [(i, i) for i in range(devices)]
+        up_own = lax.ppermute(up_slab, axes, stay)
+        down_own = lax.ppermute(down_slab, axes, stay)
 
     send, coef = pl.pallas_call(
         dispatch_kernel,
@@ -199,28 +191,25 @@
         return rows.reshape(2 * slots * LANE_BLOCKS, part)
 
     received = exchange(send)
-    slab_shapes = [pltpu.VMEM(w.shape, BF16) for w in (gate_slab, up_slab, down_slab)]
     partial = pl.pallas_call(
         experts_kernel,
         out_shape=pltpu.VMEM((2 * slots * LANE_BLOCKS, part), BF16),
-        in_specs=[vmem] * 4 + [anywhere] * 3,
+        in_specs=[vmem] * 7,
         out_specs=vmem,
-        scratch_shapes=slab_shapes
-        + [
+        scratch_shapes=[
             pltpu.VMEM((2 * slots, width), BF16),
             pltpu.VMEM((2, 2 * slots, slab), BF16),
-            pltpu.SemaphoreType.DMA((3,)),
         ],
-        compiler_params=pltpu.CompilerParams(vmem_limit_bytes=30 * MIB),
+        compiler_params=pltpu.CompilerParams(vmem_limit_bytes=11 * MIB),
         name="experts",
     )(
         in_vmem(received),
+        in_vmem(gate_slab),
+        in_vmem(up_own),
+        in_vmem(down_own),
         in_vmem(gate_other),
         in_vmem(up_other),
         in_vmem(down_other),
-        in_hbm(gate_slab),
-        in_hbm(up_slab),
-        in_hbm(down_slab),
     )
 
     returned = exchange(partial)

time: 160 us -> 161 us (level)
  starting transfers between devices: 0.51 us -> 6.58 us
  Pallas kernels: 29.4 us -> 24.6 us
    ppermute x0 -> x2, starting transfers between devices: none -> 5.8 us  [the longest x1 2.97 us: on_device(): up_own = lax.ppermute(up_slab, axes, stay)]
    pallas_call x1, Pallas kernels: 22.2 us -> 17.5 us  [on_device(): pl.pallas_call(experts_kernel, out_shape=pltpu.VMEM((2 * slots * LANE_BLO...]
  transfers between devices with their start and end apart: 3 -> 5, of which waited for: 0 -> 0; matrix products, arithmetic and copies ran while one was open for 0% -> 0% of each run, Pallas kernels for 2% -> 2%
where the time goes in v3:
time: 161 us
  blocking collectives  129 us (80%)
  Pallas kernels  24.6 us (15%)
  starting transfers between devices  6.58 us (4%)
    all_to_all x2, blocking collectives, exchange(): lax.all_to_all(rows, axes, 0, 0, axis_index_groups=same_core, tiled=True)  129 us
    pallas_call x1, Pallas kernels, on_device(): pl.pallas_call(experts_kernel, out_shape=pltpu.VMEM((2 * slots * LANE_BLO...  17.5 us
    pallas_call x1, Pallas kernels, on_device(): pl.pallas_call(dispatch_kernel, out_shape=(pltpu.VMEM((2, slots * LANE_BL...  3.8 us
    pallas_call x1, Pallas kernels, on_device(): pl.pallas_call(combine_kernel, out_shape=jax.ShapeDtypeStruct((toks, widt...  3.32 us
  transfers between devices with their start and end apart: 5, of which 0 were waited for; matrix products, arithmetic and copies ran while one was open for 0% of the time, Pallas kernels for 2%

profile of v3, /device:TPU:0, one launch (start us, length us, event | category | flops | bytes accessed | tf_op | source)
XLA Modules:
  0.0 160.9 jit_solution(11888930641018060347)
XLA Ops:
  0.0 0.0 copy-start
  0.0 0.0 collective-permute-start.3
  0.0 3.0 %collective-permute-start = (bf16[448,7168]{1,0:T(8,128)(2,1)}, bf16[448,7168]{1,0:T(8,128)(2,1)S(1)}, u32[]{:S(2)}, u32[]{:S(2)}) collective-permute-start(bf16[448,7168]{1,0:T(8,128)(2,1)} %bitcast.22), channel_id=1, source_target_pairs={{0,0},{1,1},{2,2},{3,3},{4,4},{5,5},{6,6},{7,7},{8,8},{9,9},{10,10... | collective-permute-start | bytes 19267592 | tf_op jit(solution)/shard_map/sibling_weights/ppermute | solution.py:165
  3.0 0.8 collective-permute-start.2
  3.8 0.0 collective-permute-start.4
  3.8 2.8 %collective-permute-start.1 = (bf16[448,7168]{1,0:T(8,128)(2,1)}, bf16[448,7168]{1,0:T(8,128)(2,1)S(1)}, u32[]{:S(2)}, u32[]{:S(2)}) collective-permute-start(bf16[448,7168]{1,0:T(8,128)(2,1)} %bitcast.24), channel_id=1, source_target_pairs={{0,0},{1,1},{2,2},{3,3},{4,4},{5,5},{6,6},{7,7},{8,8},{9,9},{10,10... | collective-permute-start | bytes 19267592 | tf_op jit(solution)/shard_map/sibling_weights/ppermute | solution.py:166
  6.6 3.8 %dispatch.1 = (bf16[2,1280,896]{2,1,0:T(8,128)(2,1)S(1)}, bf16[128,160]{1,0:T(8,128)(2,1)S(1)}) custom-call(s32[384]{0:T(512)} %limits_ref.1, s32[8,128]{1,0:T(8,128)} %bitcast.19, bf16[8,128]{1,0:T(8,128)(2,1)} %bitcast.20, bf16[128,7168]{1,0:T(8,128)(2,1)} %tokens_hbm.1), custom_call_target="tpu_custom_call" | custom-call | tf_op jit(solution)/shard_map/dispatch/pallas_call | solution.py:168
  10.4 68.6 %all_to_all.10 = bf16[64,40,896]{2,1,0:T(8,128)(2,1)S(1)} all-to-all(bf16[64,40,896]{2,1,0:T(8,128)(2,1)S(1)} %bitcast.18), channel_id=1, replica_groups={{0,4,8,12,16,20,24,28,32,36,40,44,48,52,56,60,64,68,72,76,80,84,88,92,9..., dimensions={0} | all-to-all | bytes 9175040 | tf_op jit(solution)/shard_map/all_to_all | solution.py:190
  79.0 0.0 collective-permute-done.2.g1
  79.0 0.0 collective-permute-done.3.u1
  79.0 0.0 collective-permute-done.u0
  79.0 0.0 collective-permute-done.4.d1
  79.0 0.0 collective-permute-done.1.d0
  79.0 0.0 copy-done
  79.0 17.5 %experts.1 = bf16[2560,896]{1,0:T(8,128)(2,1)S(1)} custom-call(bf16[2560,896]{1,0:T(8,128)(2,1)S(1)} %bitcast.13, bf16[448,7168]{1,0:T(8,128)(2,1)S(1)} %bitcast.17, bf16[448,7168]{1,0:T(8,128)(2,1)S(1)} %collective-permute-done.u0, bf16[448,7168]{1,0:T(8,128)(2,1)S(1)} %collective-permute-done.1.d0, bf16[448,7168]{1,0:T(8,128)(2,1)S(1)} %collective-permute-done.2.g1, ...), custom_call_target="tpu_custom_call" | custom-call | tf_op jit(solution)/shard_map/experts/pallas_call | solution.py:194
  96.5 60.9 %all_to_all.11 = bf16[64,40,896]{2,1,0:T(8,128)(2,1)S(1)} all-to-all(bf16[64,40,896]{2,1,0:T(8,128)(2,1)S(1)} %bitcast.14), channel_id=1, replica_groups={{0,4,8,12,16,20,24,28,32,36,40,44,48,52,56,60,64,68,72,76,80,84,88,92,9..., dimensions={0} | all-to-all | bytes 9175040 | tf_op jit(solution)/shard_map/all_to_all | solution.py:190
  157.4 3.3 %combine.1 = bf16[128,7168]{1,0:T(8,128)(2,1)} custom-call(bf16[128,160]{1,0:T(8,128)(2,1)S(1)} %get-tuple-element.7.coef_ref, bf16[2560,896]{1,0:T(8,128)(2,1)S(1)} %bitcast.15), custom_call_target="tpu_custom_call" | custom-call | tf_op jit(solution)/shard_map/combine/pallas_call | solution.py:216
Async XLA Ops:
  0.0 79.0 %copy-start = (bf16[1,7168,448]{1,2,0:T(8,128)(2,1)S(1)}, bf16[1,7168,448]{1,2,0:T(8,128)(2,1)}, u32[]{:S(2)}) copy-start(bf16[1,7168,448]{1,2,0:T(8,128)(2,1)} %param.11) | copy-start | bytes 19267588
  0.0 79.0 %collective-permute-start.3 = (bf16[448,7168]{1,0:T(8,128)(2,1)}, bf16[448,7168]{1,0:T(8,128)(2,1)S(1)}, u32[]{:S(2)}, u32[]{:S(2)}) collective-permute-start(bf16[448,7168]{1,0:T(8,128)(2,1)} %bitcast.21), channel_id=1, source_target_pairs={{0,1},{1,0},{2,3},{3,2},{4,5},{5,4},{6,7},{7,6},{8,9},{9,8},{10,11... | collective-permute-start | bytes 19267592 | tf_op jit(solution)/shard_map/sibling_weights/ppermute | solution.py:162
  0.0 79.0 %collective-permute-start = (bf16[448,7168]{1,0:T(8,128)(2,1)}, bf16[448,7168]{1,0:T(8,128)(2,1)S(1)}, u32[]{:S(2)}, u32[]{:S(2)}) collective-permute-start(bf16[448,7168]{1,0:T(8,128)(2,1)} %bitcast.22), channel_id=1, source_target_pairs={{0,0},{1,1},{2,2},{3,3},{4,4},{5,5},{6,6},{7,7},{8,8},{9,9},{10,10... | collective-permute-start | bytes 19267592 | tf_op jit(solution)/shard_map/sibling_weights/ppermute | solution.py:165
  3.0 76.0 %collective-permute-start.2 = (bf16[448,7168]{1,0:T(8,128)(2,1)}, bf16[448,7168]{1,0:T(8,128)(2,1)S(1)}, u32[]{:S(2)}, u32[]{:S(2)}) collective-permute-start(bf16[448,7168]{1,0:T(8,128)(2,1)} %bitcast.16), channel_id=1, source_target_pairs={{0,1},{1,0},{2,3},{3,2},{4,5},{5,4},{6,7},{7,6},{8,9},{9,8},{10,11... | collective-permute-start | bytes 19267592 | tf_op jit(solution)/shard_map/sibling_weights/ppermute | solution.py:161
  3.8 75.3 %collective-permute-start.4 = (bf16[448,7168]{1,0:T(8,128)(2,1)}, bf16[448,7168]{1,0:T(8,128)(2,1)S(1)}, u32[]{:S(2)}, u32[]{:S(2)}) collective-permute-start(bf16[448,7168]{1,0:T(8,128)(2,1)} %bitcast.23), channel_id=1, source_target_pairs={{0,1},{1,0},{2,3},{3,2},{4,5},{5,4},{6,7},{7,6},{8,9},{9,8},{10,11... | collective-permute-start | bytes 19267592 | tf_op jit(solution)/shard_map/sibling_weights/ppermute | solution.py:163
  3.8 75.3 %collective-permute-start.1 = (bf16[448,7168]{1,0:T(8,128)(2,1)}, bf16[448,7168]{1,0:T(8,128)(2,1)S(1)}, u32[]{:S(2)}, u32[]{:S(2)}) collective-permute-start(bf16[448,7168]{1,0:T(8,128)(2,1)} %bitcast.24), channel_id=1, source_target_pairs={{0,0},{1,1},{2,2},{3,3},{4,4},{5,5},{6,6},{7,7},{8,8},{9,9},{10,10... | collective-permute-start | bytes 19267592 | tf_op jit(solution)/shard_map/sibling_weights/ppermute | solution.py:166

commit v4 on v3

--- a/solution.py
+++ b/solution.py
@@ -51,10 +51,12 @@
 
 
 def dispatch_kernel(
-    limits_ref, ids_ref, gates_ref, tokens_hbm, send_ref, coef_ref, tokens_ref, rows_ref, tokens_sem
+    limits_ref, ids_ref, gates_ref, tokens_hbm, up_hbm, send_ref, coef_ref, up_ref, tokens_ref, rows_ref, sem
 ):
-    fetch = pltpu.make_async_copy(tokens_hbm, tokens_ref, tokens_sem)
+    fetch = pltpu.make_async_copy(tokens_hbm, tokens_ref, sem.at[0])
     fetch.start()
+    fetch_up = pltpu.make_async_copy(up_hbm, up_ref, sem.at[1])
+    fetch_up.start()
     toks, width = tokens_ref.shape
     slots = rows_ref.shape[0]
     experts = slots // CAP
@@ -95,6 +97,7 @@
         for h in range(2):
             send_ref[h, g * size : (g + 1) * size, :] = packed
     coef_ref[...] = jnp.where(taken, slot_gate, 0.0).T.astype(BF16)
+    fetch_up.wait()
 
 
 def experts_kernel(x_ref, g0, u0, d0, g1, u1, d1, y_ref, rows_ref, hidden_ref):
@@ -161,26 +164,24 @@
         gate_other = lax.ppermute(gate_slab, axes, swap)
         up_other = lax.ppermute(up_slab, axes, swap)
         down_other = lax.ppermute(down_slab, axes, swap)
-        stay = [(i, i) for i in range(devices)]
-        up_own = lax.ppermute(up_slab, axes, stay)
-        down_own = lax.ppermute(down_slab, axes, stay)
-
-    send, coef = pl.pallas_call(
+
+    send, coef, up_own = pl.pallas_call(
         dispatch_kernel,
         out_shape=(
             pltpu.VMEM((2, slots * LANE_BLOCKS, part), BF16),
             pltpu.VMEM((toks, slots), BF16),
+            pltpu.VMEM((slab, width), BF16),
         ),
-        in_specs=[smem, vmem, vmem, anywhere],
-        out_specs=(vmem, vmem),
+        in_specs=[smem, vmem, vmem, anywhere, anywhere],
+        out_specs=(vmem, vmem, vmem),
         scratch_shapes=[
             pltpu.VMEM((toks, width), BF16),
             pltpu.VMEM((slots, width), BF16),
-            pltpu.SemaphoreType.DMA,
+            pltpu.SemaphoreType.DMA((2,)),
         ],
         compiler_params=pltpu.CompilerParams(vmem_limit_bytes=8 * MIB),
         name="dispatch",
-    )(in_hbm(limits), in_hbm(route_ids.T), in_hbm(route_gates.T), in_hbm(tokens))
+    )(in_hbm(limits), in_hbm(route_ids.T), in_hbm(route_gates.T), in_hbm(tokens), in_hbm(up_slab))
 
     order = [2 * (2 * e + h) for h in range(2) for e in range(hosted)]
     same_core = [[i + c for i in order] for c in range(2)]
@@ -206,7 +207,7 @@
         in_vmem(received),
         in_vmem(gate_slab),
         in_vmem(up_own),
-        in_vmem(down_own),
+        in_vmem(down_slab),
         in_vmem(gate_other),
         in_vmem(up_other),
         in_vmem(down_other),

time: 161 us -> 156 us (0.969)
  starting transfers between devices: 6.58 us -> 0.51 us
    ppermute x2 -> x0, starting transfers between devices: 5.8 us -> none  [the longest x1 2.97 us: on_device(): up_own = lax.ppermute(up_slab, axes, stay)]
  transfers between devices with their start and end apart: 5 -> 3, of which waited for: 0 -> 0; matrix products, arithmetic and copies ran while one was open for 0% -> 0% of each run, Pallas kernels for 2% -> 3%
where the time goes in v4:
time: 156 us
  blocking collectives  130 us (83%)
  Pallas kernels  25.3 us (16%)
    all_to_all x2, blocking collectives, exchange(): lax.all_to_all(rows, axes, 0, 0, axis_index_groups=same_core, tiled=True)  130 us
    pallas_call x1, Pallas kernels, on_device(): pl.pallas_call(experts_kernel, out_shape=pltpu.VMEM((2 * slots * LANE_BLO...  17.5 us
    pallas_call x1, Pallas kernels, on_device(): pl.pallas_call(dispatch_kernel, out_shape=(pltpu.VMEM((2, slots * LANE_BL...  4.51 us
    pallas_call x1, Pallas kernels, on_device(): pl.pallas_call(combine_kernel, out_shape=jax.ShapeDtypeStruct((toks, widt...  3.32 us
  transfers between devices with their start and end apart: 3, of which 0 were waited for; matrix products, arithmetic and copies ran while one was open for 0% of the time, Pallas kernels for 3%

profile of v4, /device:TPU:0, one launch (start us, length us, event | category | flops | bytes accessed | tf_op | source)
XLA Modules:
  0.0 156.2 jit_solution(268115038166041136)
XLA Ops:
  0.0 0.0 collective-permute-start
  0.0 0.5 collective-permute-start.1
  0.5 0.0 collective-permute-start.2
  0.5 0.0 slice-start
  0.5 4.5 %dispatch.1 = (bf16[2,1280,896]{2,1,0:T(8,128)(2,1)S(1)}, bf16[128,160]{1,0:T(8,128)(2,1)S(1)}, bf16[448,7168]{1,0:T(8,128)(2,1)S(1)}) custom-call(s32[384]{0:T(512)} %limits_ref.1, s32[8,128]{1,0:T(8,128)} %bitcast.25, bf16[8,128]{1,0:T(8,128)(2,1)} %bitcast.26, bf16[128,7168]{1,0:T(8,128)(2,1)} %tokens_hbm.1, bf16[448,7168]{1,0:T(8,128)(2,1)} %bitcast.24), custom_call_target="tpu_custom_call" | custom-call | tf_op jit(solution)/shard_map/dispatch/pallas_call | solution.py:168
  5.0 0.0 copy-start
  5.0 0.0 slice-start.1
  5.1 69.0 %all_to_all.10 = bf16[64,40,896]{2,1,0:T(8,128)(2,1)S(1)} all-to-all(bf16[64,40,896]{2,1,0:T(8,128)(2,1)S(1)} %bitcast.22), channel_id=1, replica_groups={{0,4,8,12,16,20,24,28,32,36,40,44,48,52,56,60,64,68,72,76,80,84,88,92,9..., dimensions={0} | all-to-all | bytes 9175040 | tf_op jit(solution)/shard_map/all_to_all | solution.py:191
  74.1 0.0 collective-permute-done.g1
  74.1 0.0 collective-permute-done.1.u1
  74.1 0.0 collective-permute-done.2.d1
  74.1 0.0 slice-done
  74.1 0.0 copy-done
  74.1 0.0 slice-done.1
  74.1 17.5 %experts.1 = bf16[2560,896]{1,0:T(8,128)(2,1)S(1)} custom-call(bf16[2560,896]{1,0:T(8,128)(2,1)S(1)} %bitcast.13, bf16[448,7168]{1,0:T(8,128)(2,1)S(1)} %bitcast.19, bf16[448,7168]{1,0:T(8,128)(2,1)S(1)} %get-tuple-element.10.u0, bf16[448,7168]{1,0:T(8,128)(2,1)S(1)} %bitcast.21, bf16[448,7168]{1,0:T(8,128)(2,1)S(1)} %collective-permute-done.g1, ...), custom_call_target="tpu_custom_call" | custom-call | tf_op jit(solution)/shard_map/experts/pallas_call | solution.py:195
  91.6 61.1 %all_to_all.11 = bf16[64,40,896]{2,1,0:T(8,128)(2,1)S(1)} all-to-all(bf16[64,40,896]{2,1,0:T(8,128)(2,1)S(1)} %bitcast.14), channel_id=1, replica_groups={{0,4,8,12,16,20,24,28,32,36,40,44,48,52,56,60,64,68,72,76,80,84,88,92,9..., dimensions={0} | all-to-all | bytes 9175040 | tf_op jit(solution)/shard_map/all_to_all | solution.py:191
  152.7 3.3 %combine.1 = bf16[128,7168]{1,0:T(8,128)(2,1)} custom-call(bf16[128,160]{1,0:T(8,128)(2,1)S(1)} %get-tuple-element.8.coef_ref, bf16[2560,896]{1,0:T(8,128)(2,1)S(1)} %bitcast.15), custom_call_target="tpu_custom_call" | custom-call | tf_op jit(solution)/shard_map/combine/pallas_call | solution.py:217
  (1 shorter events, 0.0 us)
Async XLA Ops:
  0.0 74.1 %collective-permute-start = (bf16[448,7168]{1,0:T(8,128)(2,1)}, bf16[448,7168]{1,0:T(8,128)(2,1)S(1)}, u32[]{:S(2)}, u32[]{:S(2)}) collective-permute-start(bf16[448,7168]{1,0:T(8,128)(2,1)} %bitcast.16), channel_id=1, source_target_pairs={{0,1},{1,0},{2,3},{3,2},{4,5},{5,4},{6,7},{7,6},{8,9},{9,8},{10,11... | collective-permute-start | bytes 19267592 | tf_op jit(solution)/shard_map/sibling_weights/ppermute | solution.py:164
  0.0 74.1 %collective-permute-start.1 = (bf16[448,7168]{1,0:T(8,128)(2,1)}, bf16[448,7168]{1,0:T(8,128)(2,1)S(1)}, u32[]{:S(2)}, u32[]{:S(2)}) collective-permute-start(bf16[448,7168]{1,0:T(8,128)(2,1)} %bitcast.23), channel_id=1, source_target_pairs={{0,1},{1,0},{2,3},{3,2},{4,5},{5,4},{6,7},{7,6},{8,9},{9,8},{10,11... | collective-permute-start | bytes 19267592 | tf_op jit(solution)/shard_map/sibling_weights/ppermute | solution.py:165
  0.5 73.6 %collective-permute-start.2 = (bf16[448,7168]{1,0:T(8,128)(2,1)}, bf16[448,7168]{1,0:T(8,128)(2,1)S(1)}, u32[]{:S(2)}, u32[]{:S(2)}) collective-permute-start(bf16[448,7168]{1,0:T(8,128)(2,1)} %bitcast.20), channel_id=1, source_target_pairs={{0,1},{1,0},{2,3},{3,2},{4,5},{5,4},{6,7},{7,6},{8,9},{9,8},{10,11... | collective-permute-start | bytes 19267592 | tf_op jit(solution)/shard_map/sibling_weights/ppermute | solution.py:166
  0.5 73.6 %slice-start = ((s8[6422528]{0:T(1024)(128)(4,1)}), s8[4194304]{0:T(1024)(128)(4,1)S(1)}, s32[]{:S(2)}) async-start(s8[6422528]{0:T(1024)(128)(4,1)} %bitcast.17), calls=%async_computation.2 | async-start | bytes 8388608
  5.0 69.0 %copy-start = (bf16[1,448,7168]{2,1,0:T(8,128)(2,1)S(1)}, bf16[1,448,7168]{2,1,0:T(8,128)(2,1)}, u32[]{:S(2)}) copy-start(bf16[1,448,7168]{2,1,0:T(8,128)(2,1)} %param.13) | copy-start | bytes 19267588
  5.0 69.0 %slice-start.1 = ((s8[6422528]{0:T(1024)(128)(4,1)}), s8[2228224]{0:T(1024)(128)(4,1)S(1)}, s32[]{:S(2)}) async-start(s8[6422528]{0:T(1024)(128)(4,1)} %bitcast.17), calls=%async_computation.3 | async-start | bytes 4456448

commit v5 on v4

--- a/solution.py
+++ b/solution.py
@@ -33,21 +33,38 @@
     return (src == want).astype(BF16)
 
 
-def unpack_rows(shuffle, packed, rows_ref, g):
-    part = packed.shape[1]
-    flat = jnp.dot(shuffle, packed, preferred_element_type=F32).astype(BF16)
-    at = g * BUNDLE
-    for b in range(LANE_BLOCKS):
-        rows_ref[at : at + BUNDLE, b * part : (b + 1) * part] = flat[b * BUNDLE : (b + 1) * BUNDLE]
-
-
-def pack_rows(shuffle, rows_ref, g):
+def groups_of_two(count):
+    return [range(g, min(g + 2, count)) for g in range(0, count, 2)]
+
+
+def unpack_all(packed_ref, rows_ref):
+    part = packed_ref.shape[1]
+    size = BUNDLE * LANE_BLOCKS
+    shuffle = shuffle_matrix(False)
+    for group in groups_of_two(rows_ref.shape[0] // BUNDLE):
+        packed = jnp.concatenate([packed_ref[g * size : (g + 1) * size, :] for g in group], axis=1)
+        flat = jnp.dot(shuffle, packed, preferred_element_type=F32).astype(BF16)
+        for i, g in enumerate(group):
+            for b in range(LANE_BLOCKS):
+                rows_ref[g * BUNDLE : (g + 1) * BUNDLE, b * part : (b + 1) * part] = flat[
+                    b * BUNDLE : (b + 1) * BUNDLE, i * part : (i + 1) * part
+                ]
+
+
+def pack_all(rows_ref, store):
     part = rows_ref.shape[1] // LANE_BLOCKS
-    at = g * BUNDLE
-    stacked = jnp.concatenate(
-        [rows_ref[at : at + BUNDLE, b * part : (b + 1) * part] for b in range(LANE_BLOCKS)], axis=0
-    )
-    return jnp.dot(shuffle, stacked, preferred_element_type=F32).astype(BF16)
+    size = BUNDLE * LANE_BLOCKS
+    shuffle = shuffle_matrix(True)
+    for group in groups_of_two(rows_ref.shape[0] // BUNDLE):
+        stacked = [
+            jnp.concatenate(
+                [rows_ref[g * BUNDLE : (g + 1) * BUNDLE, b * part : (b + 1) * part] for b in range(LANE_BLOCKS)], axis=0
+            )
+            for g in group
+        ]
+        packed = jnp.dot(shuffle, jnp.concatenate(stacked, axis=1), preferred_element_type=F32).astype(BF16)
+        for i, g in enumerate(group):
+            store(slice(g * size, (g + 1) * size), packed[:, i * part : (i + 1) * part])
 
 
 def dispatch_kernel(
@@ -90,23 +107,19 @@
         rows_ref[:, at : at + step] = jnp.dot(
             pick, tokens_ref[:, at : at + step], preferred_element_type=F32
         ).astype(BF16)
-    shuffle = shuffle_matrix(True)
-    size = BUNDLE * LANE_BLOCKS
-    for g in range(slots // BUNDLE):
-        packed = pack_rows(shuffle, rows_ref, g)
+
+    def store(at, packed):
         for h in range(2):
-            send_ref[h, g * size : (g + 1) * size, :] = packed
+            send_ref[h, at, :] = packed
+
+    pack_all(rows_ref, store)
     coef_ref[...] = jnp.where(taken, slot_gate, 0.0).T.astype(BF16)
     fetch_up.wait()
 
 
 def experts_kernel(x_ref, g0, u0, d0, g1, u1, d1, y_ref, rows_ref, hidden_ref):
-    rows, width = rows_ref.shape
-    size = BUNDLE * LANE_BLOCKS
-    bundles = rows // BUNDLE
-    shuffle = shuffle_matrix(False)
-    for g in range(bundles):
-        unpack_rows(shuffle, x_ref[g * size : (g + 1) * size, :], rows_ref, g)
+    width = rows_ref.shape[1]
+    unpack_all(x_ref, rows_ref)
     across = (((1,), (1,)), ((), ()))
 
     def slab_hidden(gate_w, up_w):
@@ -121,16 +134,15 @@
         total = jnp.dot(hidden_ref[0], d0[:, at : at + step], preferred_element_type=F32)
         total += jnp.dot(hidden_ref[1], d1[:, at : at + step], preferred_element_type=F32)
         rows_ref[:, at : at + step] = total.astype(BF16)
-    back = shuffle_matrix(True)
-    for g in range(bundles):
-        y_ref[g * size : (g + 1) * size, :] = pack_rows(back, rows_ref, g)
+
+    def store(at, packed):
+        y_ref[at, :] = packed
+
+    pack_all(rows_ref, store)
 
 
 def combine_kernel(coef_ref, y_ref, out_hbm, out_ref, rows_ref, sem):
-    size = BUNDLE * LANE_BLOCKS
-    shuffle = shuffle_matrix(False)
-    for g in range(rows_ref.shape[0] // BUNDLE):
-        unpack_rows(shuffle, y_ref[g * size : (g + 1) * size, :], rows_ref, g)
+    unpack_all(y_ref, rows_ref)
     half = rows_ref.shape[0] // 2
     step = 1024
     copies = []

time: 156 us -> 156 us (level)
  no operation moved by 1% of the time
where the time goes in v5:
time: 156 us
  blocking collectives  130 us (83%)
  Pallas kernels  24.8 us (16%)
    all_to_all x2, blocking collectives, exchange(): lax.all_to_all(rows, axes, 0, 0, axis_index_groups=same_core, tiled=True)  130 us
    pallas_call x1, Pallas kernels, on_device(): pl.pallas_call(experts_kernel, out_shape=pltpu.VMEM((2 * slots * LANE_BLO...  17.1 us
    pallas_call x1, Pallas kernels, on_device(): pl.pallas_call(dispatch_kernel, out_shape=(pltpu.VMEM((2, slots * LANE_BL...  4.51 us
    pallas_call x1, Pallas kernels, on_device(): pl.pallas_call(combine_kernel, out_shape=jax.ShapeDtypeStruct((toks, widt...  3.22 us
  transfers between devices with their start and end apart: 3, of which 0 were waited for; matrix products, arithmetic and copies ran while one was open for 0% of the time, Pallas kernels for 3%

profile of v5, /device:TPU:0, one launch (start us, length us, event | category | flops | bytes accessed | tf_op | source)
XLA Modules:
  0.0 155.7 jit_solution(8991795716872614745)
XLA Ops:
  0.0 0.0 collective-permute-start
  0.0 0.5 collective-permute-start.1
  0.5 0.0 collective-permute-start.2
  0.5 0.0 slice-start
  0.5 4.5 %dispatch.1 = (bf16[2,1280,896]{2,1,0:T(8,128)(2,1)S(1)}, bf16[128,160]{1,0:T(8,128)(2,1)S(1)}, bf16[448,7168]{1,0:T(8,128)(2,1)S(1)}) custom-call(s32[384]{0:T(512)} %limits_ref.1, s32[8,128]{1,0:T(8,128)} %bitcast.25, bf16[8,128]{1,0:T(8,128)(2,1)} %bitcast.26, bf16[128,7168]{1,0:T(8,128)(2,1)} %tokens_hbm.1, bf16[448,7168]{1,0:T(8,128)(2,1)} %bitcast.24), custom_call_target="tpu_custom_call" | custom-call | tf_op jit(solution)/shard_map/dispatch/pallas_call | solution.py:180
  5.0 0.0 copy-start
  5.0 0.0 slice-start.1
  5.1 69.0 %all_to_all.10 = bf16[64,40,896]{2,1,0:T(8,128)(2,1)S(1)} all-to-all(bf16[64,40,896]{2,1,0:T(8,128)(2,1)S(1)} %bitcast.22), channel_id=1, replica_groups={{0,4,8,12,16,20,24,28,32,36,40,44,48,52,56,60,64,68,72,76,80,84,88,92,9..., dimensions={0} | all-to-all | bytes 9175040 | tf_op jit(solution)/shard_map/all_to_all | solution.py:203
  74.1 0.0 collective-permute-done.g1
  74.1 0.0 collective-permute-done.1.u1
  74.1 0.0 collective-permute-done.2.d1
  74.1 0.0 slice-done
  74.1 0.0 copy-done
  74.1 0.0 slice-done.1
  74.1 17.1 %experts.1 = bf16[2560,896]{1,0:T(8,128)(2,1)S(1)} custom-call(bf16[2560,896]{1,0:T(8,128)(2,1)S(1)} %bitcast.13, bf16[448,7168]{1,0:T(8,128)(2,1)S(1)} %bitcast.19, bf16[448,7168]{1,0:T(8,128)(2,1)S(1)} %get-tuple-element.10.u0, bf16[448,7168]{1,0:T(8,128)(2,1)S(1)} %bitcast.21, bf16[448,7168]{1,0:T(8,128)(2,1)S(1)} %collective-permute-done.g1, ...), custom_call_target="tpu_custom_call" | custom-call | tf_op jit(solution)/shard_map/experts/pallas_call | solution.py:207
  91.2 61.1 %all_to_all.11 = bf16[64,40,896]{2,1,0:T(8,128)(2,1)S(1)} all-to-all(bf16[64,40,896]{2,1,0:T(8,128)(2,1)S(1)} %bitcast.14), channel_id=1, replica_groups={{0,4,8,12,16,20,24,28,32,36,40,44,48,52,56,60,64,68,72,76,80,84,88,92,9..., dimensions={0} | all-to-all | bytes 9175040 | tf_op jit(solution)/shard_map/all_to_all | solution.py:203
  152.3 3.2 %combine.1 = bf16[128,7168]{1,0:T(8,128)(2,1)} custom-call(bf16[128,160]{1,0:T(8,128)(2,1)S(1)} %get-tuple-element.8.coef_ref, bf16[2560,896]{1,0:T(8,128)(2,1)S(1)} %bitcast.15), custom_call_target="tpu_custom_call" | custom-call | tf_op jit(solution)/shard_map/combine/pallas_call | solution.py:229
  (1 shorter events, 0.0 us)
Async XLA Ops:
  0.0 74.1 %collective-permute-start = (bf16[448,7168]{1,0:T(8,128)(2,1)}, bf16[448,7168]{1,0:T(8,128)(2,1)S(1)}, u32[]{:S(2)}, u32[]{:S(2)}) collective-permute-start(bf16[448,7168]{1,0:T(8,128)(2,1)} %bitcast.16), channel_id=1, source_target_pairs={{0,1},{1,0},{2,3},{3,2},{4,5},{5,4},{6,7},{7,6},{8,9},{9,8},{10,11... | collective-permute-start | bytes 19267592 | tf_op jit(solution)/shard_map/sibling_weights/ppermute | solution.py:176
  0.0 74.1 %collective-permute-start.1 = (bf16[448,7168]{1,0:T(8,128)(2,1)}, bf16[448,7168]{1,0:T(8,128)(2,1)S(1)}, u32[]{:S(2)}, u32[]{:S(2)}) collective-permute-start(bf16[448,7168]{1,0:T(8,128)(2,1)} %bitcast.23), channel_id=1, source_target_pairs={{0,1},{1,0},{2,3},{3,2},{4,5},{5,4},{6,7},{7,6},{8,9},{9,8},{10,11... | collective-permute-start | bytes 19267592 | tf_op jit(solution)/shard_map/sibling_weights/ppermute | solution.py:177
  0.5 73.6 %collective-permute-start.2 = (bf16[448,7168]{1,0:T(8,128)(2,1)}, bf16[448,7168]{1,0:T(8,128)(2,1)S(1)}, u32[]{:S(2)}, u32[]{:S(2)}) collective-permute-start(bf16[448,7168]{1,0:T(8,128)(2,1)} %bitcast.20), channel_id=1, source_target_pairs={{0,1},{1,0},{2,3},{3,2},{4,5},{5,4},{6,7},{7,6},{8,9},{9,8},{10,11... | collective-permute-start | bytes 19267592 | tf_op jit(solution)/shard_map/sibling_weights/ppermute | solution.py:178
  0.5 73.6 %slice-start = ((s8[6422528]{0:T(1024)(128)(4,1)}), s8[4194304]{0:T(1024)(128)(4,1)S(1)}, s32[]{:S(2)}) async-start(s8[6422528]{0:T(1024)(128)(4,1)} %bitcast.17), calls=%async_computation.2 | async-start | bytes 8388608
  5.0 69.0 %copy-start = (bf16[1,448,7168]{2,1,0:T(8,128)(2,1)S(1)}, bf16[1,448,7168]{2,1,0:T(8,128)(2,1)}, u32[]{:S(2)}) copy-start(bf16[1,448,7168]{2,1,0:T(8,128)(2,1)} %param.13) | copy-start | bytes 19267588
  5.0 69.0 %slice-start.1 = ((s8[6422528]{0:T(1024)(128)(4,1)}), s8[2228224]{0:T(1024)(128)(4,1)S(1)}, s32[]{:S(2)}) async-start(s8[6422528]{0:T(1024)(128)(4,1)} %bitcast.17), calls=%async_computation.3 | async-start | bytes 4456448

commit v6 on v5

--- a/solution.py
+++ b/solution.py
@@ -68,12 +68,37 @@
 
 
 def dispatch_kernel(
-    limits_ref, ids_ref, gates_ref, tokens_hbm, up_hbm, send_ref, coef_ref, up_ref, tokens_ref, rows_ref, sem
+    limits_hbm,
+    ids_hbm,
+    gates_hbm,
+    tokens_hbm,
+    up_hbm,
+    send_ref,
+    coef_ref,
+    up_ref,
+    limits_ref,
+    ids_ref,
+    gates_ref,
+    tokens_ref,
+    rows_ref,
+    sem,
 ):
-    fetch = pltpu.make_async_copy(tokens_hbm, tokens_ref, sem.at[0])
-    fetch.start()
-    fetch_up = pltpu.make_async_copy(up_hbm, up_ref, sem.at[1])
-    fetch_up.start()
+    fetches = [
+        pltpu.make_async_copy(source, place, sem.at[i])
+        for i, (source, place) in enumerate(
+            (
+                (ids_hbm, ids_ref),
+                (gates_hbm, gates_ref),
+                (limits_hbm, limits_ref),
+                (tokens_hbm, tokens_ref),
+                (up_hbm, up_ref),
+            )
+        )
+    ]
+    for fetch in fetches:
+        fetch.start()
+    for fetch in fetches[:3]:
+        fetch.wait()
     toks, width = tokens_ref.shape
     slots = rows_ref.shape[0]
     experts = slots // CAP
@@ -101,7 +126,7 @@
     place = lax.rem(lax.broadcasted_iota(jnp.int32, (slots, toks), 0), CAP).astype(F32) + 1.0
     taken = slot_rank == place
     pick = jnp.where(taken, 1.0, 0.0).astype(BF16)
-    fetch.wait()
+    fetches[3].wait()
     step = 1024
     for at in range(0, width, step):
         rows_ref[:, at : at + step] = jnp.dot(
@@ -114,7 +139,7 @@
 
     pack_all(rows_ref, store)
     coef_ref[...] = jnp.where(taken, slot_gate, 0.0).T.astype(BF16)
-    fetch_up.wait()
+    fetches[4].wait()
 
 
 def experts_kernel(x_ref, g0, u0, d0, g1, u1, d1, y_ref, rows_ref, hidden_ref):
@@ -167,7 +192,6 @@
     slots = hosted * CAP
     part = width // LANE_BLOCKS
     vmem = pl.BlockSpec(memory_space=pltpu.VMEM)
-    smem = pl.BlockSpec(memory_space=pltpu.SMEM)
     anywhere = pl.BlockSpec(memory_space=pl.ANY)
 
     gate_slab, up_slab, down_slab = w_gate[0].T, w_up[0].T, w_down[0]
@@ -184,12 +208,15 @@
             pltpu.VMEM((toks, slots), BF16),
             pltpu.VMEM((slab, width), BF16),
         ),
-        in_specs=[smem, vmem, vmem, anywhere, anywhere],
+        in_specs=[anywhere] * 5,
         out_specs=(vmem, vmem, vmem),
         scratch_shapes=[
+            pltpu.SMEM(limits.shape, jnp.int32),
+            pltpu.VMEM(route_ids.shape[::-1], jnp.int32),
+            pltpu.VMEM(route_gates.shape[::-1], BF16),
             pltpu.VMEM((toks, width), BF16),
             pltpu.VMEM((slots, width), BF16),
-            pltpu.SemaphoreType.DMA((2,)),
+            pltpu.SemaphoreType.DMA((5,)),
         ],
         compiler_params=pltpu.CompilerParams(vmem_limit_bytes=8 * MIB),
         name="dispatch",

time: 156 us -> 155 us (level)
  transfers between devices with their start and end apart: 3 -> 3, of which waited for: 0 -> 0; matrix products, arithmetic and copies ran while one was open for 0% -> 0% of each run, Pallas kernels for 3% -> 2%
where the time goes in v6:
time: 155 us
  blocking collectives  130 us (84%)
  Pallas kernels  23.9 us (15%)
    all_to_all x2, blocking collectives, exchange(): lax.all_to_all(rows, axes, 0, 0, axis_index_groups=same_core, tiled=True)  130 us
    pallas_call x1, Pallas kernels, on_device(): pl.pallas_call(experts_kernel, out_shape=pltpu.VMEM((2 * slots * LANE_BLO...  17.1 us
    pallas_call x1, Pallas kernels, on_device(): pl.pallas_call(dispatch_kernel, out_shape=(pltpu.VMEM((2, slots * LANE_BL...  3.6 us
    pallas_call x1, Pallas kernels, on_device(): pl.pallas_call(combine_kernel, out_shape=jax.ShapeDtypeStruct((toks, widt...  3.22 us
  transfers between devices with their start and end apart: 3, of which 0 were waited for; matrix products, arithmetic and copies ran while one was open for 0% of the time, Pallas kernels for 2%

profile of v6, /device:TPU:0, one launch (start us, length us, event | category | flops | bytes accessed | tf_op | source)
XLA Modules:
  0.0 154.8 jit_solution(6985307009774293208)
XLA Ops:
  0.0 0.0 collective-permute-start
  0.0 0.5 collective-permute-start.1
  0.5 0.0 collective-permute-start.2
  0.5 0.0 slice-start
  0.5 3.6 %dispatch.1 = (bf16[2,1280,896]{2,1,0:T(8,128)(2,1)S(1)}, bf16[128,160]{1,0:T(8,128)(2,1)S(1)}, bf16[448,7168]{1,0:T(8,128)(2,1)S(1)}) custom-call(s32[384]{0:T(512)} %limits_hbm.1, s32[8,128]{1,0:T(8,128)} %bitcast.25, bf16[8,128]{1,0:T(8,128)(2,1)} %bitcast.26, bf16[128,7168]{1,0:T(8,128)(2,1)} %tokens_hbm.1, bf16[448,7168]{1,0:T(8,128)(2,1)} %bitcast.24), custom_call_target="tpu_custom_call" | custom-call | tf_op jit(solution)/shard_map/dispatch/pallas_call | solution.py:204
  4.1 0.0 copy-start
  4.1 0.0 slice-start.1
  4.1 69.0 %all_to_all.10 = bf16[64,40,896]{2,1,0:T(8,128)(2,1)S(1)} all-to-all(bf16[64,40,896]{2,1,0:T(8,128)(2,1)S(1)} %bitcast.22), channel_id=1, replica_groups={{0,4,8,12,16,20,24,28,32,36,40,44,48,52,56,60,64,68,72,76,80,84,88,92,9..., dimensions={0} | all-to-all | bytes 9175040 | tf_op jit(solution)/shard_map/all_to_all | solution.py:230
  73.1 0.0 collective-permute-done.g1
  73.1 0.0 collective-permute-done.1.u1
  73.2 0.0 collective-permute-done.2.d1
  73.2 0.0 slice-done
  73.2 0.0 copy-done
  73.2 0.0 slice-done.1
  73.2 17.1 %experts.1 = bf16[2560,896]{1,0:T(8,128)(2,1)S(1)} custom-call(bf16[2560,896]{1,0:T(8,128)(2,1)S(1)} %bitcast.13, bf16[448,7168]{1,0:T(8,128)(2,1)S(1)} %bitcast.19, bf16[448,7168]{1,0:T(8,128)(2,1)S(1)} %get-tuple-element.10.u0, bf16[448,7168]{1,0:T(8,128)(2,1)S(1)} %bitcast.21, bf16[448,7168]{1,0:T(8,128)(2,1)S(1)} %collective-permute-done.g1, ...), custom_call_target="tpu_custom_call" | custom-call | tf_op jit(solution)/shard_map/experts/pallas_call | solution.py:234
  90.3 61.1 %all_to_all.11 = bf16[64,40,896]{2,1,0:T(8,128)(2,1)S(1)} all-to-all(bf16[64,40,896]{2,1,0:T(8,128)(2,1)S(1)} %bitcast.14), channel_id=1, replica_groups={{0,4,8,12,16,20,24,28,32,36,40,44,48,52,56,60,64,68,72,76,80,84,88,92,9..., dimensions={0} | all-to-all | bytes 9175040 | tf_op jit(solution)/shard_map/all_to_all | solution.py:230
  151.4 3.2 %combine.1 = bf16[128,7168]{1,0:T(8,128)(2,1)} custom-call(bf16[128,160]{1,0:T(8,128)(2,1)S(1)} %get-tuple-element.8.coef_ref, bf16[2560,896]{1,0:T(8,128)(2,1)S(1)} %bitcast.15), custom_call_target="tpu_custom_call" | custom-call | tf_op jit(solution)/shard_map/combine/pallas_call | solution.py:256
  (1 shorter events, 0.0 us)
Async XLA Ops:
  0.0 73.1 %collective-permute-start = (bf16[448,7168]{1,0:T(8,128)(2,1)}, bf16[448,7168]{1,0:T(8,128)(2,1)S(1)}, u32[]{:S(2)}, u32[]{:S(2)}) collective-permute-start(bf16[448,7168]{1,0:T(8,128)(2,1)} %bitcast.16), channel_id=1, source_target_pairs={{0,1},{1,0},{2,3},{3,2},{4,5},{5,4},{6,7},{7,6},{8,9},{9,8},{10,11... | collective-permute-start | bytes 19267592 | tf_op jit(solution)/shard_map/sibling_weights/ppermute | solution.py:200
  0.0 73.1 %collective-permute-start.1 = (bf16[448,7168]{1,0:T(8,128)(2,1)}, bf16[448,7168]{1,0:T(8,128)(2,1)S(1)}, u32[]{:S(2)}, u32[]{:S(2)}) collective-permute-start(bf16[448,7168]{1,0:T(8,128)(2,1)} %bitcast.23), channel_id=1, source_target_pairs={{0,1},{1,0},{2,3},{3,2},{4,5},{5,4},{6,7},{7,6},{8,9},{9,8},{10,11... | collective-permute-start | bytes 19267592 | tf_op jit(solution)/shard_map/sibling_weights/ppermute | solution.py:201
  0.5 72.6 %collective-permute-start.2 = (bf16[448,7168]{1,0:T(8,128)(2,1)}, bf16[448,7168]{1,0:T(8,128)(2,1)S(1)}, u32[]{:S(2)}, u32[]{:S(2)}) collective-permute-start(bf16[448,7168]{1,0:T(8,128)(2,1)} %bitcast.20), channel_id=1, source_target_pairs={{0,1},{1,0},{2,3},{3,2},{4,5},{5,4},{6,7},{7,6},{8,9},{9,8},{10,11... | collective-permute-start | bytes 19267592 | tf_op jit(solution)/shard_map/sibling_weights/ppermute | solution.py:202
  0.5 72.6 %slice-start = ((s8[6422528]{0:T(1024)(128)(4,1)}), s8[4194304]{0:T(1024)(128)(4,1)S(1)}, s32[]{:S(2)}) async-start(s8[6422528]{0:T(1024)(128)(4,1)} %bitcast.17), calls=%async_computation.2 | async-start | bytes 8388608
  4.1 69.0 %copy-start = (bf16[1,448,7168]{2,1,0:T(8,128)(2,1)S(1)}, bf16[1,448,7168]{2,1,0:T(8,128)(2,1)}, u32[]{:S(2)}) copy-start(bf16[1,448,7168]{2,1,0:T(8,128)(2,1)} %param.13) | copy-start | bytes 19267588
  4.1 69.0 %slice-start.1 = ((s8[6422528]{0:T(1024)(128)(4,1)}), s8[2228224]{0:T(1024)(128)(4,1)S(1)}, s32[]{:S(2)}) async-start(s8[6422528]{0:T(1024)(128)(4,1)} %bitcast.17), calls=%async_computation.3 | async-start | bytes 4456448
